TPU v7x, 32 devices: a whole 2x2x4 slice. The times are simulated.
32 devices in a mesh: section: 2 (over core), dp: 16 (over z, y, x).
Axes of the slice: x: 2, y: 2, z: 4, core: 2. Of those that a mesh axis runs over, the one named last changes fastest.
Arguments:
- tokens: bfloat16 [32, 512, 384], P('dp'), may hold values from -6 to 6
- sample_ids: int32 [32, 512], P('dp'), may hold values from 0 to 3, never falling along the last dimension, each value on 1 to 256 neighbouring positions
- cotangent: bfloat16 [32, 512, 384], P('dp'), may hold values from -6 to 6
- first_gain: float32 [2, 384], P('section'), may hold values from 0.5 to 1.5
- query_weight: bfloat16 [2, 384, 384], P('section'), may hold values from -0.3125 to 0.3125
- key_weight: bfloat16 [2, 384, 384], P('section'), may hold values from -0.3125 to 0.3125
- value_weight: bfloat16 [2, 384, 384], P('section'), may hold values from -0.3125 to 0.3125
- output_weight: bfloat16 [2, 384, 384], P('section'), may hold values from -2.5 to 2.5
- second_gain: float32 [2, 384], P('section'), may hold values from 0.5 to 1.5
- gate_weight: bfloat16 [2, 384, 1024], P('section'), may hold values from -0.3125 to 0.3125
- up_weight: bfloat16 [2, 384, 1024], P('section'), may hold values from -0.3125 to 0.3125
- down_weight: bfloat16 [2, 1024, 384], P('section'), may hold values from -0.1875 to 0.1875
Outputs:
- layer_outputs: bfloat16 [2, 32, 512, 384], P('section', 'dp')
- input_grads: float32 [2, 32, 512, 384], P('section', 'dp')
- first_gain_grad: float32 [2, 384], P('section')
- query_grad: float32 [2, 384, 384], P('section')
- key_grad: float32 [2, 384, 384], P('section')
- value_grad: float32 [2, 384, 384], P('section')
- output_grad: float32 [2, 384, 384], P('section')
- second_gain_grad: float32 [2, 384], P('section')
- gate_grad: float32 [2, 384, 1024], P('section')
- up_grad: float32 [2, 384, 1024], P('section')
- down_grad: float32 [2, 1024, 384], P('section')
Inputs may be any that keep to these rules, and one draw needn't show every extreme that they name: `sample_ids`: within each row the ids never fall; a token attends only to tokens of its own row with the same id; each id covers 1 to 256 positions of a row and one covers exactly 256.
All inputs are finite; a program needn't handle non-finite values.
Results may differ from a plain program's by a relative error of at most 0.02.
Values may be sent and summed in bfloat16 or wider, within the bound.
A program may use at most 128 MiB of HBM per device.

v0:
```python
import jax
import jax.numpy as jnp
from jax import lax
from jax.sharding import PartitionSpec as P

HEADS = 6
HEAD_DIM = 64
MICRO = 2


NORM_EPS = 1e-05
MASKED = -1e30


def shifted(block, axis, distance):
    devices = range(lax.axis_size(axis))
    route = [(i - distance, i) for i in devices if i - distance in devices]
    return lax.ppermute(block, axis, route)


def matmul(left, right):
    return jnp.dot(left, right, preferred_element_type=jnp.float32)


def left_trans(left, right):
    return lax.dot_general(
        left, right, (((0,), (0,)), ((), ())), preferred_element_type=jnp.float32
    )


def right_trans(left, right):
    return lax.dot_general(
        left, right, (((1,), (1,)), ((), ())), preferred_element_type=jnp.float32
    )


def norm_parts(values):
    scale_row = lax.rsqrt(jnp.mean(values * values, axis=-1, keepdims=True) + NORM_EPS)
    return (values * scale_row, scale_row)


def back_norm(grad_normed, normed_vals, scale_row):
    return scale_row * (
        grad_normed - normed_vals * jnp.mean(grad_normed * normed_vals, axis=-1, keepdims=True)
    )


def row_scores(queries, keys_in, row_ids):
    scores = jnp.einsum(
        "qhd,khd->hqk", queries, keys_in, preferred_element_type=jnp.float32
    ) * HEAD_DIM ** (-0.5)
    same = (row_ids[:, None] == row_ids[None, :])[None]
    return jnp.where(same, scores, MASKED)


def attend_row(pieces):
    queries, keys_in, values_in, row_ids = pieces
    scores = row_scores(queries, keys_in, row_ids)
    top_score = jnp.max(scores, axis=-1, keepdims=True)
    expo = jnp.exp(scores - top_score)
    total = jnp.sum(expo, axis=-1, keepdims=True)
    probs = (expo / total).astype(jnp.bfloat16)
    mixed = jnp.einsum("hqk,khd->qhd", probs, values_in, preferred_element_type=jnp.float32).astype(
        jnp.bfloat16
    )
    return (mixed, (top_score + jnp.log(total))[..., 0])


def attend_back(pieces):
    queries, keys_in, values_in, row_ids, logsum, grad_mixed = pieces
    scale_qk = HEAD_DIM ** (-0.5)
    probs = jnp.exp(row_scores(queries, keys_in, row_ids) - logsum[..., None])
    grad_values = jnp.einsum(
        "hqk,qhd->khd", probs.astype(jnp.bfloat16), grad_mixed, preferred_element_type=jnp.float32
    ).astype(jnp.bfloat16)
    grad_probs = jnp.einsum(
        "qhd,khd->hqk", grad_mixed, values_in, preferred_element_type=jnp.float32
    )
    grad_scores = (
        probs * (grad_probs - jnp.sum(probs * grad_probs, axis=-1, keepdims=True))
    ).astype(jnp.bfloat16)
    grad_queries = (
        jnp.einsum("hqk,khd->qhd", grad_scores, keys_in, preferred_element_type=jnp.float32)
        * scale_qk
    ).astype(jnp.bfloat16)
    grad_keys = (
        jnp.einsum("hqk,qhd->khd", grad_scores, queries, preferred_element_type=jnp.float32)
        * scale_qk
    ).astype(jnp.bfloat16)
    return (grad_queries, grad_keys, grad_values)


def run_layer(inputs, row_ids, weights):
    (
        first_gain,
        query_weight,
        key_weight,
        value_weight,
        output_weight,
        second_gain,
        gate_weight,
        up_weight,
        down_weight,
    ) = weights
    width = inputs.shape[1]
    split = (row_ids.shape[0], row_ids.shape[1], HEADS, HEAD_DIM)
    attn_norm, attn_scale = norm_parts(inputs)
    attn_in = (attn_norm * first_gain).astype(jnp.bfloat16)
    queries = matmul(attn_in, query_weight).astype(jnp.bfloat16).reshape(split)
    keys_in = matmul(attn_in, key_weight).astype(jnp.bfloat16).reshape(split)
    values_in = matmul(attn_in, value_weight).astype(jnp.bfloat16).reshape(split)
    mixed, logsum = lax.map(attend_row, (queries, keys_in, values_in, row_ids))
    mixed_flat = mixed.reshape(-1, width)
    after_attn = inputs + matmul(mixed_flat, output_weight)
    ffn_norm, ffn_scale = norm_parts(after_attn)
    ffn_in = (ffn_norm * second_gain).astype(jnp.bfloat16)
    gate_act = matmul(ffn_in, gate_weight)
    up_act = matmul(ffn_in, up_weight)
    sigmoid_gate = jax.nn.sigmoid(gate_act)
    silu_gate = gate_act * sigmoid_gate
    hidden = (silu_gate * up_act).astype(jnp.bfloat16)
    result = after_attn + matmul(hidden, down_weight)
    kept = (
        attn_norm,
        attn_scale,
        attn_in,
        queries,
        keys_in,
        values_in,
        mixed_flat,
        logsum,
        ffn_norm,
        ffn_scale,
        ffn_in,
        gate_act,
        up_act,
        sigmoid_gate,
        silu_gate,
        hidden,
    )
    return (result, kept)


def back_layer(kept, row_ids, grad_out, weights):
    (
        first_gain,
        query_weight,
        key_weight,
        value_weight,
        output_weight,
        second_gain,
        gate_weight,
        up_weight,
        down_weight,
    ) = weights
    (
        attn_norm,
        attn_scale,
        attn_in,
        queries,
        keys_in,
        values_in,
        mixed_flat,
        logsum,
        ffn_norm,
        ffn_scale,
        ffn_in,
        gate_act,
        up_act,
        sigmoid_gate,
        silu_gate,
        hidden,
    ) = kept
    width = grad_out.shape[1]
    grad_low = grad_out.astype(jnp.bfloat16)
    grad_down = left_trans(hidden, grad_low)
    grad_hidden = right_trans(grad_low, down_weight)
    grad_gate_act = (
        grad_hidden * up_act * sigmoid_gate * (1.0 + gate_act * (1.0 - sigmoid_gate))
    ).astype(jnp.bfloat16)
    grad_up_act = (grad_hidden * silu_gate).astype(jnp.bfloat16)
    grad_gate = left_trans(ffn_in, grad_gate_act)
    grad_up = left_trans(ffn_in, grad_up_act)
    grad_ffn_in = right_trans(grad_gate_act, gate_weight) + right_trans(grad_up_act, up_weight)
    grad_second = jnp.sum(grad_ffn_in * ffn_norm, axis=0)
    grad_after = grad_out + back_norm(grad_ffn_in * second_gain, ffn_norm, ffn_scale)
    grad_attn_low = grad_after.astype(jnp.bfloat16)
    grad_output = left_trans(mixed_flat, grad_attn_low)
    grad_mixed = (
        right_trans(grad_attn_low, output_weight).astype(jnp.bfloat16).reshape(queries.shape)
    )
    grad_queries, grad_keys, grad_values = lax.map(
        attend_back, (queries, keys_in, values_in, row_ids, logsum, grad_mixed)
    )
    grad_queries = grad_queries.reshape(-1, width)
    grad_keys = grad_keys.reshape(-1, width)
    grad_values = grad_values.reshape(-1, width)
    grad_query = left_trans(attn_in, grad_queries)
    grad_key = left_trans(attn_in, grad_keys)
    grad_value = left_trans(attn_in, grad_values)
    grad_attn_in = (
        right_trans(grad_queries, query_weight)
        + right_trans(grad_keys, key_weight)
        + right_trans(grad_values, value_weight)
    )
    grad_first = jnp.sum(grad_attn_in * attn_norm, axis=0)
    grad_inputs = grad_after + back_norm(grad_attn_in * first_gain, attn_norm, attn_scale)
    return (
        grad_inputs,
        (
            grad_first,
            grad_query,
            grad_key,
            grad_value,
            grad_output,
            grad_second,
            grad_gate,
            grad_up,
            grad_down,
        ),
    )


def final_total(grads):
    (
        grad_first,
        grad_query,
        grad_key,
        grad_value,
        grad_output,
        grad_second,
        grad_gate,
        grad_up,
        grad_down,
    ) = grads
    return lax.psum(
        (
            grad_first,
            grad_query,
            grad_key,
            grad_value,
            grad_output,
            grad_second,
            grad_gate,
            grad_up,
            grad_down,
        ),
        "dp",
    )


def per_device(
    tokens,
    sample_ids,
    cotangent,
    first_gain,
    query_weight,
    key_weight,
    value_weight,
    output_weight,
    second_gain,
    gate_weight,
    up_weight,
    down_weight,
):
    weights = (
        first_gain[0],
        query_weight[0],
        key_weight[0],
        value_weight[0],
        output_weight[0],
        second_gain[0],
        gate_weight[0],
        up_weight[0],
        down_weight[0],
    )
    is_first = lax.axis_index("section") == 0
    rows_mb = tokens.shape[0] // MICRO
    seq_len = tokens.shape[1]
    width = tokens.shape[2]

    def rows_of(array, which):
        return array[which * rows_mb : (which + 1) * rows_mb]

    incoming = jnp.zeros((rows_mb, seq_len, width), jnp.bfloat16)
    sent_list = []
    input_list = []
    ids_list = []
    for moment in range(MICRO + 1):
        own_batch = min(moment, MICRO - 1)
        earlier = max(moment - 1, 0)
        layer_input = jnp.where(is_first, rows_of(tokens, own_batch), incoming)
        row_ids = jnp.where(is_first, rows_of(sample_ids, own_batch), rows_of(sample_ids, earlier))
        result, unused = run_layer(
            layer_input.astype(jnp.float32).reshape(-1, width), row_ids, weights
        )
        sent = result.astype(jnp.bfloat16).reshape(rows_mb, seq_len, width)
        sent_list.append(sent)
        input_list.append(layer_input)
        ids_list.append(row_ids)
        if moment < MICRO:
            incoming = shifted(sent, "section", 1)
    section_inputs = [
        jnp.where(is_first, input_list[index], input_list[index + 1]) for index in range(MICRO)
    ]
    section_ids = [
        jnp.where(is_first, ids_list[index], ids_list[index + 1]) for index in range(MICRO)
    ]
    layer_outputs = jnp.concatenate(
        [jnp.where(is_first, sent_list[index], sent_list[index + 1]) for index in range(MICRO)],
        axis=0,
    )
    returned = jnp.zeros((rows_mb, seq_len, width), jnp.bfloat16)
    totals = None
    grad_list = []
    for moment in range(MICRO + 1):
        later = min(moment, MICRO - 1)
        earlier = max(moment - 1, 0)
        if moment < MICRO:
            from_loss = rows_of(cotangent, later).astype(jnp.float32)
        else:
            from_loss = jnp.zeros((rows_mb, seq_len, width), jnp.float32)
        upstream = jnp.where(is_first, returned.astype(jnp.float32), from_loss)
        layer_input = jnp.where(is_first, section_inputs[earlier], section_inputs[later]).astype(
            jnp.float32
        )
        row_ids = jnp.where(is_first, section_ids[earlier], section_ids[later])
        unused, kept = run_layer(layer_input.reshape(-1, width), row_ids, weights)
        grad_inputs, grads = back_layer(kept, row_ids, upstream.reshape(-1, width), weights)
        grad_sent = grad_inputs.astype(jnp.bfloat16).reshape(rows_mb, seq_len, width)
        grad_list.append(
            jnp.where(
                is_first,
                grad_inputs.reshape(rows_mb, seq_len, width),
                grad_sent.astype(jnp.float32),
            )
        )
        if moment < MICRO:
            returned = shifted(grad_sent, "section", -1)
        if totals is None:
            totals = grads
        else:
            totals = tuple((accum + extra for accum, extra in zip(totals, grads)))
    totals = final_total(totals)
    input_grads = jnp.concatenate(
        [jnp.where(is_first, grad_list[index + 1], grad_list[index]) for index in range(MICRO)],
        axis=0,
    )
    return (
        layer_outputs[None],
        input_grads[None],
        totals[0][None],
        totals[1][None],
        totals[2][None],
        totals[3][None],
        totals[4][None],
        totals[5][None],
        totals[6][None],
        totals[7][None],
        totals[8][None],
    )


def solution(mesh):
    placed = (
        P("dp", None, None),
        P("dp", None),
        P("dp", None, None),
        P("section", None),
        P("section", None, None),
        P("section", None, None),
        P("section", None, None),
        P("section", None, None),
        P("section", None),
        P("section", None, None),
        P("section", None, None),
        P("section", None, None),
    )
    return jax.shard_map(
        per_device,
        mesh=mesh,
        in_specs=placed,
        out_specs=(
            P("section", "dp", None, None),
            P("section", "dp", None, None),
            P("section", None),
            P("section", None, None),
            P("section", None, None),
            P("section", None, None),
            P("section", None, None),
            P("section", None),
            P("section", None, None),
            P("section", None, None),
            P("section", None, None),
        ),
        check_vma=False,
    )
```

profile of v0, /device:TPU:0, one launch (start us, length us, event | category | flops | bytes accessed | tf_op | source)
XLA Modules:
  0.0 438.9 jit_solution(931096488803229103)
XLA Ops:
  7.3 1.3 fusion.312
  9.6 1.4 convolution_convert_fusion.18
  13.6 5.1 %fusion.313 = (f32[6,512]{1,0:T(8,128)S(1)}, f32[6,512,512]{1,2,0:T(8,128)}) fusion(pred[512,512]{0,1:T(8,128)(4,1)S(1)} %broadcast_compare_fusion.5, bf16[512,6,64]{0,2,1:T(8,128)(2,1)S(1)} %bitcast.594, bf16[512,6,64]{0,2,1:T(8,128)(2,1)S(1)} %bitcast.593), kind=kOutput, calls=%fused_computation.442 | convolution fusion | flops 207618560 | bytes 7352320 | tf_op jit(solution)/shard_map/while/body/eval_jaxpr/sub | solution.py:60
  18.7 3.5 fusion.66
  22.7 2.2 fusion.164
  24.8 4.0 fusion.45
  28.8 3.3 collective-permute-start
  39.5 2.2 convolution_convert_fusion.15
  41.7 2.2 convolution_convert_fusion.16
  43.9 2.2 convolution_convert_fusion.17
  49.7 6.3 %fusion.314 = (f32[6,512]{1,0:T(8,128)S(1)}, f32[6,512,512]{1,2,0:T(8,128)}) fusion(pred[512,512]{0,1:T(8,128)(4,1)} %broadcast_compare_fusion.4, bf16[512,6,64]{0,2,1:T(8,128)(2,1)} %bitcast.597, bf16[512,6,64]{0,2,1:T(8,128)(2,1)} %bitcast.596), kind=kOutput, calls=%fused_computation.443 | convolution fusion | flops 207618560 | bytes 7352320 | tf_op jit(solution)/shard_map/while/body/eval_jaxpr/sub | solution.py:60
  56.0 3.6 fusion.65
  60.9 2.2 fusion.162
  63.1 4.5 %fusion.46 = bf16[512,384]{0,1:T(8,128)(2,1)} fusion(f32[512,384]{0,1:T(8,128)} %copy-done.44, f32[512,1024]{1,0:T(8,128)} %fusion.162, bf16[1,1024,384]{2,1,0:T(8,128)(2,1)} %param.23, bf16[1,384,1024]{2,1,0:T(8,128)(2,1)S(1)} %copy-done.1, f32[512]{0:T(512)S(1)} %add_rsqrt_fusion.8, f32[384]{0:T(512)S(1)} %reduce.1), kind=kOutput, calls=%fused_computation.113 | convolution fusion | flops 809435136 | bytes 4853248 | tf_op jit(solution)/shard_map/dot_general | solution.py:22
  67.6 2.0 collective-permute-start.1
  69.6 2.3 fusion.317
  84.0 1.4 multiply_convert_fusion.10
  86.0 1.4 multiply_reduce_fusion.5
  89.3 4.1 multiply_reduce_fusion.2
  93.4 4.6 %multiply_convert_fusion.2 = bf16[6,512,512]{1,2,0:T(8,128)(2,1)S(1)} fusion(f32[6,512,512]{1,2,0:T(8,128)} %get-tuple-element.301, f32[6,512,512]{1,2,0:T(8,128)S(1)} %get-tuple-element.296, f32[6,512]{1,0:T(8,128)S(1)} %get-tuple-element.300, f32[6,512]{1,0:T(8,128)} %copy-done.113), kind=kLoop, calls=%fused_computation.15 | loop fusion | flops 6291456 | bytes 15753216 | tf_op jit(solution)/shard_map/while/body/eval_jaxpr/convert_element_type | solution.py:81
  98.0 2.1 fusion.40
  110.6 1.4 copy-done.81
  112.4 2.1 fusion.69
  114.8 1.7 fusion.321
  116.5 1.7 fusion.319
  123.2 1.3 collective-permute-start.2
  124.5 2.1 fusion.134
  126.7 2.1 fusion.150
  128.8 1.4 multiply_convert_fusion.8
  130.8 1.4 multiply_reduce_fusion.4
  132.8 1.9 fusion.51
  134.7 4.1 multiply_reduce_fusion.1
  138.8 4.6 %multiply_convert_fusion.1 = bf16[6,512,512]{1,2,0:T(8,128)(2,1)S(1)} fusion(f32[6,512,512]{1,2,0:T(8,128)} %get-tuple-element.309, f32[6,512,512]{1,2,0:T(8,128)S(1)} %get-tuple-element.304, f32[6,512]{1,0:T(8,128)S(1)} %get-tuple-element.308, f32[6,512]{1,0:T(8,128)S(1)} %log_add_fusion.1), kind=kLoop, calls=%fused_computation.9 | loop fusion | flops 6291456 | bytes 15753216 | tf_op jit(solution)/shard_map/while/body/eval_jaxpr/convert_element_type | solution.py:81
  143.4 2.2 fusion.42
  146.3 1.7 fusion.322
  149.9 1.4 select_bitcast_fusion.1
  151.4 1.7 collective-permute-start.3
  156.9 2.0 fusion.70
  160.2 1.7 fusion.320
  161.9 1.4 multiply_convert_fusion.6
  164.0 1.4 multiply_reduce_fusion.3
  167.1 1.3 multiply_reduce_fusion
  168.5 1.9 multiply_convert_fusion
  170.4 2.2 fusion.44
  175.3 1.8 add_bitcast_fusion.1
  178.1 1.8 add_bitcast_fusion.2
  179.9 1.5 fusion.58
  183.9 2.0 add_bitcast_fusion
  187.5 1.8 select_bitcast_fusion.2
  189.4 2.2 convolution_convert_fusion.12
  191.6 2.2 convolution_convert_fusion.13
  195.0 6.4 %fusion.315 = (f32[6,512]{1,0:T(8,128)S(1)}, f32[6,512,512]{1,2,0:T(8,128)}) fusion(pred[512,512]{0,1:T(8,128)(4,1)} %broadcast_compare_fusion.3, bf16[512,6,64]{0,2,1:T(8,128)(2,1)} %bitcast.601, bf16[512,6,64]{0,2,1:T(8,128)(2,1)} %bitcast.600), kind=kOutput, calls=%fused_computation.444 | convolution fusion | flops 207618560 | bytes 7352320 | tf_op jit(solution)/shard_map/while/body/eval_jaxpr/sub | solution.py:60
  201.4 3.6 fusion.64
  205.1 1.3 multiply_reduce_fusion.12
  206.4 3.3 fusion.160
  209.7 4.7 %fusion.68 = bf16[1,512,384]{1,2,0:T(8,128)(2,1)} fusion(bf16[512,384]{0,1:T(8,128)(2,1)} %fusion.46, f32[512,384]{0,1:T(8,128)} %get-tuple-element.290, f32[512,1024]{1,0:T(8,128)} %fusion.160, bf16[1,1024,384]{2,1,0:T(8,128)(2,1)} %param.23, bf16[1,384,1024]{2,1,0:T(8,128)(2,1)S(1)} %copy-done.1, f32[512]{0:T(512)S(1)} %add_rsqrt_fusion.6, ...), kind=kOutput, calls=%fused_computation.158 | convolution fusion | flops 809631744 | bytes 5246465 | tf_op jit(solution)/shard_map/dot_general | solution.py:22
  218.1 1.4 fusion.242
  219.5 1.4 convolution_add_fusion.1
  222.3 1.6 copy.61
  223.9 44.9 %all-reduce = (f32[1,384]{1,0:T(1,128)}, f32[1,384]{1,0:T(1,128)}) all-reduce(f32[1,384]{1,0:T(1,128)S(1)} %broadcast_in_dim.270, f32[1,384]{1,0:T(1,128)S(1)} %copy-done.123), channel_id=1, replica_groups=mesh['section'=2,'dp'=16] {'dp'}, use_global_device_ids=true, to_apply=%region_36.37 | all-reduce | flops 768 | bytes 6144 | tf_op jit(solution)/shard_map/psum | solution.py:236
  268.8 152.7 %all-reduce.4.cloned.1.call-done = (f32[1,384,384]{2,1,0:T(8,128)}, f32[1,384,384]{2,1,0:T(8,128)}, f32[1,384,384]{2,1,0:T(8,128)}, f32[1,384,384]{2,1,0:T(8,128...) async-done(((f32[1,384,384]{2,1,0:T(8,128)}, f32[1,384,384]{2,1,0:T(8,128)}, f32[1,384,384]{2,1,0:T(8,128)}, f32[1,384,384]{2,1,0:T(8,128)}, ...) | async-done | bytes 7077904 | tf_op jit(solution)/shard_map/psum | solution.py:236
  421.5 2.1 copy.106
  423.6 2.0 copy.107
  425.6 1.9 copy.108
  (385 shorter events, 75.8 us)
Async XLA Ops:
  7.2 15.5 %copy-start = (bf16[1,384,1024]{2,1,0:T(8,128)(2,1)S(1)}, bf16[1,384,1024]{2,1,0:T(8,128)(2,1)}, u32[]{:S(2)}) copy-start(bf16[1,384,1024]{2,1,0:T(8,128)(2,1)} %param.21) | copy-start | bytes 2359300
  7.2 3.9 copy-start.50
  7.2 4.3 copy-start.124
  7.2 414.3 %all-reduce.4.cloned.1.call-start = ((), (), s32[]{:S(2)}) async-start(), calls=%async_computation | async-start | bytes 14155776 | tf_op jit(solution)/shard_map/psum | solution.py:236
  7.3 5.1 %copy-start.55 = (bf16[1,384,384]{2,1,0:T(8,128)(2,1)S(1)}, bf16[1,384,384]{2,1,0:T(8,128)(2,1)}, u32[]{:S(2)}) copy-start(bf16[1,384,384]{2,1,0:T(8,128)(2,1)} %param.18) | copy-start | bytes 884740
  13.6 5.1 %copy-start.129 = (bf16[512,384]{0,1:T(8,128)(2,1)S(1)}, bf16[512,384]{0,1:T(8,128)(2,1)}, u32[]{:S(2)}) copy-start(bf16[512,384]{0,1:T(8,128)(2,1)} %convolution_convert_fusion.20) | copy-start | bytes 1179652
  18.7 3.5 copy-start.2
  18.7 4.0 copy-start.125
  28.8 10.3 %collective-permute-start = (bf16[1,512,384]{1,2,0:T(8,128)(2,1)}, bf16[1,512,384]{1,2,0:T(8,128)(2,1)}, u32[]{:S(2)}, u32[]{:S(2)}) collective-permute-start(bf16[1,512,384]{1,2,0:T(8,128)(2,1)} %bitcast.583), channel_id=1, source_target_pairs={{0,16},{1,17},{2,18},{3,19},{4,20},{5,21},{6,22},{7,23},{8,24},{9,... | collective-permute-start | bytes 1179656 | tf_op jit(solution)/shard_map/ppermute | solution.py:18
  39.1 7.0 %copy-start.51 = (bf16[1,384,384]{2,1,0:T(8,128)(2,1)S(1)}, bf16[1,384,384]{2,1,0:T(8,128)(2,1)}, u32[]{:S(2)}) copy-start(bf16[1,384,384]{2,1,0:T(8,128)(2,1)} %param.16) | copy-start | bytes 884740
  39.4 7.9 %copy-start.46 = (bf16[1,384,384]{2,1,0:T(8,128)(2,1)S(1)}, bf16[1,384,384]{2,1,0:T(8,128)(2,1)}, u32[]{:S(2)}) copy-start(bf16[1,384,384]{2,1,0:T(8,128)(2,1)} %param.17) | copy-start | bytes 884740
  39.5 9.0 %copy-start.56 = (bf16[1,384,384]{2,1,0:T(8,128)(2,1)S(1)}, bf16[1,384,384]{2,1,0:T(8,128)(2,1)}, u32[]{:S(2)}) copy-start(bf16[1,384,384]{2,1,0:T(8,128)(2,1)} %param.18) | copy-start | bytes 884740
  63.1 6.5 %copy-start.85 = (bf16[512,384]{0,1:T(8,128)(2,1)S(1)}, bf16[512,384]{0,1:T(8,128)(2,1)}, u32[]{:S(2)}) copy-start(bf16[512,384]{0,1:T(8,128)(2,1)} %convolution_convert_fusion.9) | copy-start | bytes 1179652
  67.6 7.3 %collective-permute-start.1 = (bf16[1,512,384]{1,2,0:T(8,128)(2,1)}, bf16[1,512,384]{1,2,0:T(8,128)(2,1)S(1)}, u32[]{:S(2)}, u32[]{:S(2)}) collective-permute-start(bf16[1,512,384]{1,2,0:T(8,128)(2,1)} %bitcast.584), channel_id=1, source_target_pairs={{0,16},{1,17},{2,18},{3,19},{4,20},{5,21},{6,22},{7,23},{8,24},{9,... | collective-permute-start | bytes 1179656 | tf_op jit(solution)/shard_map/ppermute | solution.py:18
  74.2 15.1 %copy-start.113 = (f32[6,512]{1,0:T(8,128)}, f32[6,512]{1,0:T(8,128)S(1)}, u32[]{:S(2)}) copy-start(f32[6,512]{1,0:T(8,128)S(1)} %log_add_fusion.2) | copy-start | bytes 36868
  89.3 12.3 %copy-start.36 = (bf16[6,64,512]{2,1,0:T(8,128)(2,1)}, bf16[6,64,512]{2,1,0:T(8,128)(2,1)S(1)}, u32[]{:S(2)}) copy-start(bf16[6,64,512]{2,1,0:T(8,128)(2,1)S(1)} %fusion.48) | copy-start | bytes 1179652
  108.8 3.1 copy-start.81
  108.8 3.1 copy-start.102
  109.6 19.1 %copy-start.74 = (f32[512,1024]{1,0:T(8,128)}, f32[512,1024]{1,0:T(8,128)S(1)}, u32[]{:S(2)}) copy-start(f32[512,1024]{1,0:T(8,128)S(1)} %fusion.137) | copy-start | bytes 6291460
  112.4 16.4 %copy-start.76 = (f32[512,1024]{1,0:T(8,128)}, f32[512,1024]{1,0:T(8,128)S(1)}, u32[]{:S(2)}) copy-start(f32[512,1024]{1,0:T(8,128)S(1)} %fusion.154) | copy-start | bytes 6291460
  114.5 3.8 copy-start.98
  116.5 2.9 copy-start.37
  118.3 6.2 %copy-start.9 = (bf16[512,384]{0,1:T(8,128)(2,1)S(1)}, bf16[512,384]{0,1:T(8,128)(2,1)}, u32[]{:S(2)}) copy-start(bf16[512,384]{0,1:T(8,128)(2,1)} %get-tuple-element.277) | copy-start | bytes 1179652
  120.7 5.9 %copy-start.115 = (f32[6,512]{1,0:T(8,128)S(1)}, f32[6,512]{1,0:T(8,128)}, u32[]{:S(2)}) copy-start(f32[6,512]{1,0:T(8,128)} %copy-done.114) | copy-start | bytes 36868
  120.7 5.9 %copy-start.117 = (f32[6,512]{1,0:T(8,128)S(1)}, f32[6,512]{1,0:T(8,128)}, u32[]{:S(2)}) copy-start(f32[6,512]{1,0:T(8,128)} %copy-done.116) | copy-start | bytes 36868
  123.2 5.5 %collective-permute-start.2 = (bf16[1,512,384]{1,2,0:T(8,128)(2,1)S(1)}, bf16[1,512,384]{1,2,0:T(8,128)(2,1)S(1)}, u32[]{:S(2)}, u32[]{:S(2)}) collective-permute-start(bf16[1,512,384]{1,2,0:T(8,128)(2,1)S(1)} %get-tuple-element.263), channel_id=1, source_target_pairs={{16,0},{17,1},{18,2},{19,3},{20,4},{21,5},{22,6},{23,7},{24,8},{25... | collective-permute-start | bytes 1179656 | tf_op jit(solution)/shard_map/ppermute | solution.py:18
  124.5 4.2 copy-start.93
  124.5 4.2 copy-start.127
  128.8 3.4 copy-start.109
  149.9 3.2 copy-start.62
  149.9 3.2 copy-start.100
  151.3 5.5 %copy-start.15 = (f32[512,384]{0,1:T(8,128)}, f32[512,384]{0,1:T(8,128)S(1)}, u32[]{:S(2)}) copy-start(f32[512,384]{0,1:T(8,128)S(1)} %get-tuple-element.224) | copy-start | bytes 2359300
  151.3 3.1 copy-start.65
  151.3 4.3 copy-start.64
  151.3 5.5 %copy-start.75 = (f32[512,1024]{1,0:T(8,128)S(1)}, f32[512,1024]{1,0:T(8,128)}, u32[]{:S(2)}) copy-start(f32[512,1024]{1,0:T(8,128)} %copy-done.74) | copy-start | bytes 6291460
  151.4 5.5 %copy-start.77 = (f32[512,1024]{1,0:T(8,128)S(1)}, f32[512,1024]{1,0:T(8,128)}, u32[]{:S(2)}) copy-start(f32[512,1024]{1,0:T(8,128)} %copy-done.76) | copy-start | bytes 6291460
  151.4 5.5 %copy-start.94 = (bf16[1,512,384]{1,2,0:T(8,128)(2,1)S(1)}, bf16[1,512,384]{1,2,0:T(8,128)(2,1)}, u32[]{:S(2)}) copy-start(bf16[1,512,384]{1,2,0:T(8,128)(2,1)} %copy.98) | copy-start | bytes 1179652
  151.4 5.5 %copy-start.110 = (bf16[1,512,384]{1,2,0:T(8,128)(2,1)S(1)}, bf16[1,512,384]{1,2,0:T(8,128)(2,1)}, u32[]{:S(2)}) copy-start(bf16[1,512,384]{1,2,0:T(8,128)(2,1)} %copy-done.109) | copy-start | bytes 1179652
  151.4 10.5 %collective-permute-start.3 = (bf16[1,512,384]{1,2,0:T(8,128)(2,1)S(1)}, bf16[1,512,384]{1,2,0:T(8,128)(2,1)S(1)}, u32[]{:S(2)}, u32[]{:S(2)}) collective-permute-start(bf16[1,512,384]{1,2,0:T(8,128)(2,1)S(1)} %convert_bitcast_fusion.6), channel_id=1, source_target_pairs={{16,0},{17,1},{18,2},{19,3},{20,4},{21,5},{22,6},{23,7},{24,8},{25... | collective-permute-start | bytes 1179656 | tf_op jit(solution)/shard_map/ppermute | solution.py:18
  156.9 3.3 copy-start.24
  158.9 3.0 copy-start.70
  158.9 3.0 copy-start.72
  158.9 3.0 copy-start.128
  161.9 3.5 copy-start.111
  167.1 12.8 %copy-start.38 = (bf16[6,64,512]{2,1,0:T(8,128)(2,1)}, bf16[6,64,512]{2,1,0:T(8,128)(2,1)S(1)}, u32[]{:S(2)}) copy-start(bf16[6,64,512]{2,1,0:T(8,128)(2,1)S(1)} %fusion.54) | copy-start | bytes 1179652
  172.5 8.8 %copy-start.43 = (bf16[6,64,512]{2,1,0:T(8,128)(2,1)}, bf16[6,64,512]{2,1,0:T(8,128)(2,1)S(1)}, u32[]{:S(2)}) copy-start(bf16[6,64,512]{2,1,0:T(8,128)(2,1)S(1)} %fusion.44) | copy-start | bytes 1179652
  173.2 9.3 %copy-start.41 = (bf16[6,64,512]{2,1,0:T(8,128)(2,1)}, bf16[6,64,512]{2,1,0:T(8,128)(2,1)S(1)}, u32[]{:S(2)}) copy-start(bf16[6,64,512]{2,1,0:T(8,128)(2,1)S(1)} %fusion.43) | copy-start | bytes 1179652
  178.1 3.3 copy-start.67
  178.1 5.8 %copy-start.130 = (f32[1024,384]{1,0:T(8,128)S(1)}, f32[1024,384]{1,0:T(8,128)}, u32[]{:S(2)}) copy-start(f32[1024,384]{1,0:T(8,128)} %fusion.69) | copy-start | bytes 4718596
  178.1 5.8 %copy-start.131 = (f32[1024,384]{1,0:T(8,128)S(1)}, f32[1024,384]{1,0:T(8,128)}, u32[]{:S(2)}) copy-start(f32[1024,384]{1,0:T(8,128)} %fusion.70) | copy-start | bytes 4718596
  179.9 4.0 copy-start.71
  179.9 4.0 copy-start.73
  179.9 4.0 copy-start.112
  185.9 3.4 copy-start.35
  185.9 7.8 %copy-start.60 = (bf16[1,384,384]{2,1,0:T(8,128)(2,1)S(1)}, bf16[1,384,384]{2,1,0:T(8,128)(2,1)}, u32[]{:S(2)}) copy-start(bf16[1,384,384]{2,1,0:T(8,128)(2,1)} %param.18) | copy-start | bytes 884740
  214.3 3.7 copy-start.42
  214.3 6.6 %copy-start.39 = (bf16[6,64,512]{2,1,0:T(8,128)(2,1)S(1)}, bf16[6,64,512]{2,1,0:T(8,128)(2,1)}, u32[]{:S(2)}) copy-start(bf16[6,64,512]{2,1,0:T(8,128)(2,1)} %copy-done.38) | copy-start | bytes 1179652
  216.8 4.2 copy-start.61
  218.1 3.4 copy-start.121
  218.1 3.4 copy-start.122
  218.1 3.5 copy-start.16
  421.5 6.0 %copy-start.105 = (f32[1,384,384]{2,1,0:T(8,128)S(1)}, f32[1,384,384]{2,1,0:T(8,128)}, u32[]{:S(2)}) copy-start(f32[1,384,384]{2,1,0:T(8,128)} %get-tuple-element.323) | copy-start | bytes 1769476
  421.5 6.8 %copy-start.92 = (f32[1,384,1024]{2,1,0:T(8,128)S(1)}, f32[1,384,1024]{2,1,0:T(8,128)}, u32[]{:S(2)}) copy-start(f32[1,384,1024]{2,1,0:T(8,128)} %get-tuple-element.325) | copy-start | bytes 4718596
  423.6 5.9 %copy-start.91 = (f32[1,384,1024]{2,1,0:T(8,128)S(1)}, f32[1,384,1024]{2,1,0:T(8,128)}, u32[]{:S(2)}) copy-start(f32[1,384,1024]{2,1,0:T(8,128)} %get-tuple-element.326) | copy-start | bytes 4718596
  (73 other events, 143.0 us)
Sparse Core Ops, SparseCore 0:
  186.1 235.4 all-reduce.3
where the time goes:
time: 445 us; the launch traced here: 439 us
  matrix products  162 us (36%)
  waiting for transfers between devices  153 us (34%)
  blocking collectives  44.9 us (10%)
  other arithmetic  29.5 us (7%)
  local copies, waits for them, and re-layouts  25.5 us (6%)
  between operations  16.4 us (4%)
  starting transfers between devices  8.36 us (2%)
    psum x1, waiting for transfers between devices, final_total(): lax.psum((grad_first, grad_query, grad_key, grad_value, grad_output, grad...  153 us
    dot_general x36, matrix products, matmul(): return jnp.dot(left, right, preferred_element_type=jnp.float32)  52.9 us
    psum x1, blocking collectives, final_total(): lax.psum((grad_first, grad_query, grad_key, grad_value, grad_output, grad...  44.9 us
    dot_general x21, matrix products, left_trans(): lax.dot_general(left, right, (((0,), (0,)), ((), ())), preferred_element_...  31.6 us
    unnamed x277, local copies, waits for them, and re-layouts  22.4 us
    dot_general x21, matrix products, right_trans(): lax.dot_general(left, right, (((1,), (1,)), ((), ())), preferred_element_...  18.3 us
    sub x3, matrix products, attend_row(): expo = jnp.exp(scores - top_score)  17.8 us
    dot_general x6, matrix products, attend_row(): jnp.einsum('hqk,khd->qhd', probs, values_in, preferred_element_type=jnp.f...  14.4 us
  transfers between devices with their start and end apart: 5, of which 1 were waited for; matrix products, arithmetic and copies ran while one was open for 14% of the time, Pallas kernels for 0%

commit v1 on v0

v1 whole, which is shorter than its diff:
```python
import functools
import types

import jax
import jax.numpy as jnp
from jax import lax
from jax.experimental import pallas as pl
from jax.experimental.pallas import tpu as pltpu
from jax.sharding import PartitionSpec as P

MESH = pl.DeviceIdType.MESH
BF = jnp.bfloat16
F32 = jnp.float32
HEADS = 6
HEAD_DIM = 64
NORM_EPS = 1e-05
MASKED = -1e30
GROUP = 16

SEQ = 512
DIM = 384
FF = 1024
HALF = SEQ // 2
CHUNK = FF // 4
UNITS = 12
UNIT = 2304
SHARE = UNIT // 2
PA = 384
PC = SHARE - 2 * PA

LANDINGS = (
    ("A1", PA // 2), ("A2", PA // 4), ("A3", PA // 4), ("A4", PA // 8),
    ("B1", PA // 2), ("B2", PA // 4), ("B3", PA // 4), ("B4", PA // 8),
    ("C1", PC), ("C2", PC // 2), ("C3", PC // 4), ("C4", PC // 8),
)
LAND = {}
LAND_ROWS = 0
for _name, _rows in LANDINGS:
    LAND[_name] = (LAND_ROWS, _rows)
    LAND_ROWS += _rows

COPIES = ["K"] + [part + str(step) for part in "ABC" for step in range(1, 9)] + ["F"]
SEM = {name: index for index, name in enumerate(COPIES)}


def mm(a, b):
    return lax.dot_general(a, b, (((1,), (0,)), ((), ())), preferred_element_type=F32)


def mm_nt(a, b):
    return lax.dot_general(a, b, (((1,), (1,)), ((), ())), preferred_element_type=F32)


def mm_tn(a, b):
    return lax.dot_general(a, b, (((0,), (0,)), ((), ())), preferred_element_type=F32)


def rsqrt_mean(values):
    return lax.rsqrt(jnp.mean(values * values, axis=-1, keepdims=True) + NORM_EPS)


def rows(start, size):
    return pl.ds(pl.multiple_of(start, 16), size)


class Links:
    def __init__(self, s):
        self.s = s
        self.c = lax.axis_index("section")
        self.dp = lax.axis_index("dp")
        local = lax.rem(self.dp, GROUP)
        self.x = lax.rem(local, 2)
        self.y = lax.rem(lax.div(local, 2), 2)
        self.z = lax.div(local, 4)
        self.middle = (self.z == 1) | (self.z == 2)
        self.end = (self.z == 0) | (self.z == 3)
        self.m = lax.div(self.z, 2)
        self.to_core = (1 - self.c, self.dp)
        self.to_x = (self.c, self.dp + 1 - 2 * self.x)
        self.to_y = (self.c, self.dp + 2 - 4 * self.y)
        self.to_pair = (self.c, self.dp + 4 - 8 * lax.rem(self.z, 2))
        self.to_middle = (self.c, self.dp + 4 - 8 * self.m)
        self.a1 = self.x * (PA // 2)
        self.a2 = self.a1 + self.y * (PA // 4)
        self.a3 = self.a2 + self.m * (PA // 8)
        self.b1 = PA + self.y * (PA // 2)
        self.b2 = self.b1 + self.x * (PA // 4)
        self.b3 = self.b2 + self.m * (PA // 8)
        self.c0 = 2 * PA
        self.c1 = self.c0 + self.m * (PC // 2)
        self.c2 = self.c1 + self.x * (PC // 4)
        self.c3 = self.c2 + self.y * (PC // 8)

    def meet(self):
        barrier = pltpu.get_barrier_semaphore()
        for target in (self.to_core, self.to_x, self.to_y, self.to_pair):
            pl.semaphore_signal(barrier, inc=1, device_id=target, device_id_type=MESH)

        @pl.when(self.middle)
        def _():
            pl.semaphore_signal(barrier, inc=1, device_id=self.to_middle, device_id_type=MESH)

    def met(self):
        barrier = pltpu.get_barrier_semaphore()

        @pl.when(self.middle)
        def _():
            pl.semaphore_wait(barrier, 5)

        @pl.when(self.end)
        def _():
            pl.semaphore_wait(barrier, 4)

    def copy(self, u, name, src, dst, target):
        return pltpu.make_async_remote_copy(
            src_ref=src,
            dst_ref=dst,
            send_sem=self.s.send.at[u, SEM[name]],
            recv_sem=self.s.recv.at[u, SEM[name]],
            device_id=target,
            device_id_type=MESH,
        )

    def down(self, u, name, start, target):
        place, size = LAND[name]
        return self.copy(
            u, name, self.s.part.at[u, rows(start, size)], self.s.land.at[u, rows(place, size)], target
        )

    def up(self, u, name, start, size, target):
        here = self.s.done.at[u, rows(start, size)]
        return self.copy(u, name, here, here, target)

    def arrived(self, u, name, start):
        place, size = LAND[name]
        self.down(u, name, start, self.to_core).wait_recv()
        here = rows(start, size)
        self.s.part[u, here] = self.s.part[u, here] + self.s.land[u, rows(place, size)]

    def finish(self, u, name, start):
        place, size = LAND[name]
        self.down(u, name, start, self.to_core).wait_recv()
        here = rows(start, size)
        self.s.done[u, here] = self.s.part[u, here] + self.s.land[u, rows(place, size)]

    def core_copy(self, u):
        return self.copy(
            u, "K", self.s.own.at[u, rows((1 - self.c) * SHARE, SHARE)], self.s.part.at[u], self.to_core
        )

    def result(self, u):
        place = lax.rem(u, 6)
        return self.s.grads_out.at[place, rows(self.c * SHARE, SHARE)]

    def result_local(self, u):
        return pltpu.make_async_copy(self.s.done.at[u], self.result(u), self.s.send.at[u, SEM["F"]])

    def result_copy(self, u):
        return self.copy(u, "F", self.s.done.at[u], self.result(u), self.to_core)

    def sends(self):
        every, middle, end = None, self.middle, self.end
        return {
            "A1": (lambda u: self.down(u, "A1", (1 - self.x) * (PA // 2), self.to_x), every),
            "A2": (lambda u: self.down(u, "A2", self.a1 + (1 - self.y) * (PA // 4), self.to_y), every),
            "A3": (lambda u: self.down(u, "A3", self.a2, self.to_pair), end),
            "A4": (lambda u: self.down(u, "A4", self.a2 + (1 - self.m) * (PA // 8), self.to_middle), middle),
            "A5": (lambda u: self.up(u, "A5", self.a3, PA // 8, self.to_middle), middle),
            "A6": (lambda u: self.up(u, "A6", self.a2, PA // 4, self.to_pair), middle),
            "A7": (lambda u: self.up(u, "A7", self.a2, PA // 4, self.to_y), every),
            "A8": (lambda u: self.up(u, "A8", self.a1, PA // 2, self.to_x), every),
            "B1": (lambda u: self.down(u, "B1", PA + (1 - self.y) * (PA // 2), self.to_y), every),
            "B2": (lambda u: self.down(u, "B2", self.b1 + (1 - self.x) * (PA // 4), self.to_x), every),
            "B3": (lambda u: self.down(u, "B3", self.b2, self.to_pair), end),
            "B4": (lambda u: self.down(u, "B4", self.b2 + (1 - self.m) * (PA // 8), self.to_middle), middle),
            "B5": (lambda u: self.up(u, "B5", self.b3, PA // 8, self.to_middle), middle),
            "B6": (lambda u: self.up(u, "B6", self.b2, PA // 4, self.to_pair), middle),
            "B7": (lambda u: self.up(u, "B7", self.b2, PA // 4, self.to_x), every),
            "B8": (lambda u: self.up(u, "B8", self.b1, PA // 2, self.to_y), every),
            "C1": (lambda u: self.down(u, "C1", self.c0, self.to_pair), end),
            "C2": (lambda u: self.down(u, "C2", self.c0 + (1 - self.m) * (PC // 2), self.to_middle), middle),
            "C3": (lambda u: self.down(u, "C3", self.c1 + (1 - self.x) * (PC // 4), self.to_x), middle),
            "C4": (lambda u: self.down(u, "C4", self.c2 + (1 - self.y) * (PC // 8), self.to_y), middle),
            "C5": (lambda u: self.up(u, "C5", self.c3, PC // 8, self.to_y), middle),
            "C6": (lambda u: self.up(u, "C6", self.c2, PC // 4, self.to_x), middle),
            "C7": (lambda u: self.up(u, "C7", self.c1, PC // 2, self.to_middle), middle),
            "C8": (lambda u: self.up(u, "C8", self.c0, PC, self.to_pair), middle),
        }

    def stage(self, step, u):
        table = self.sends()

        def start(*names):
            for name in names:
                table[name][0](u).start()

        def landed(name, size, at):
            self.up(u, name, at, size, self.to_core).wait_recv()

        if step == 0:
            self.core_copy(u).wait_recv()
            mine = rows(self.c * SHARE, SHARE)
            self.s.part[u] = self.s.part[u] + self.s.own[u, mine]
            start("A1", "B1")
            pl.when(self.end)(lambda: start("C1"))
        elif step == 1:
            self.arrived(u, "A1", self.a1)
            start("A2")
            self.arrived(u, "B1", self.b1)
            start("B2")

            @pl.when(self.middle)
            def _():
                self.arrived(u, "C1", self.c0)
                start("C2")
        elif step == 2:
            self.arrived(u, "A2", self.a2)
            self.arrived(u, "B2", self.b2)
            pl.when(self.end)(lambda: start("A3", "B3"))

            @pl.when(self.middle)
            def _():
                self.arrived(u, "C2", self.c1)
                start("C3")
        elif step == 3:

            @pl.when(self.middle)
            def _():
                self.arrived(u, "A3", self.a2)
                start("A4")
                self.arrived(u, "B3", self.b2)
                start("B4")
                self.arrived(u, "C3", self.c2)
                start("C4")
        elif step == 4:

            @pl.when(self.middle)
            def _():
                self.finish(u, "A4", self.a3)
                start("A5")
                self.finish(u, "B4", self.b3)
                start("B5")
                self.finish(u, "C4", self.c3)
                start("C5")
        elif step == 5:

            @pl.when(self.middle)
            def _():
                landed("A5", PA // 8, self.a3)
                start("A6", "A7")
                landed("B5", PA // 8, self.b3)
                start("B6", "B7")
                landed("C5", PC // 8, self.c3)
                start("C6")
        elif step == 6:

            @pl.when(self.end)
            def _():
                landed("A6", PA // 4, self.a2)
                start("A7")
                landed("B6", PA // 4, self.b2)
                start("B7")

            @pl.when(self.middle)
            def _():
                landed("C6", PC // 4, self.c2)
                start("C7")
        elif step == 7:
            landed("A7", PA // 4, self.a2)
            start("A8")
            landed("B7", PA // 4, self.b2)
            start("B8")

            @pl.when(self.middle)
            def _():
                landed("C7", PC // 2, self.c1)
                start("C8")
        elif step == 8:
            landed("A8", PA // 2, self.a1)
            landed("B8", PA // 2, self.b1)

            @pl.when(self.end)
            def _():
                landed("C8", PC, self.c0)

            layer = 1 - lax.div(u, 6)
            pl.when(layer == self.c)(lambda: self.result_local(u).start())
            pl.when(layer != self.c)(lambda: self.result_copy(u).start())

    def settle(self, u):
        self.core_copy(u).wait_send()
        for make, who in self.sends().values():
            if who is None:
                make(u).wait_send()
            else:
                pl.when(who)(lambda make=make: make(u).wait_send())
        layer = 1 - lax.div(u, 6)

        @pl.when(layer == self.c)
        def _():
            self.result_local(u).wait()
            self.result_copy(u).wait_recv()

        @pl.when(layer != self.c)
        def _():
            self.result_copy(u).wait_send()

    def sum_gains(self):
        s = self.s
        total = s.gain_sum

        def copy(index, target):
            return pltpu.make_async_remote_copy(
                src_ref=total.at[index],
                dst_ref=s.gain_land.at[index],
                send_sem=s.gain_send.at[index],
                recv_sem=s.gain_recv.at[index],
                device_id=target,
                device_id_type=MESH,
            )

        for index, target in enumerate((self.to_core, self.to_x, self.to_y)):
            one = copy(index, target)
            one.start()
            one.wait_recv()
            total[index + 1] = total[index] + s.gain_land[index]

        @pl.when(self.end)
        def _():
            copy(3, self.to_pair).start()
            copy(5, self.to_pair).wait_recv()
            total[6] = s.gain_land[5]

        @pl.when(self.middle)
        def _():
            copy(3, self.to_pair).wait_recv()
            total[4] = total[3] + s.gain_land[3]
            copy(4, self.to_middle).start()
            copy(4, self.to_middle).wait_recv()
            total[5] = total[4] + s.gain_land[4]
            copy(5, self.to_pair).start()
            total[6] = total[5]

        for index in range(3):
            copy(index, self.to_core).wait_send()

        @pl.when(self.end)
        def _():
            copy(3, self.to_pair).wait_send()

        @pl.when(self.middle)
        def _():
            copy(4, self.to_middle).wait_send()
            copy(5, self.to_pair).wait_send()


WEIGHTS = ("first_gain", "query", "key", "value", "output", "second_gain", "gate", "up", "down")


def kernel(names, lag, *refs):
    s = types.SimpleNamespace(**dict(zip(names, refs)))
    links = Links(s)
    c = links.c
    links.meet()

    token_copy = pltpu.make_async_copy(s.tokens.at[c], s.tok, s.in_sem.at[0])
    token_copy.start()
    cot_copy = pltpu.make_async_copy(s.cotangent.at[c], s.cot, s.in_sem.at[1])
    cot_copy.start()

    def place(name, layer):
        where = {
            "first_gain": lambda: s.gain1.at[layer],
            "query": lambda: s.wqkv.at[layer, :, pl.ds(0, DIM)],
            "key": lambda: s.wqkv.at[layer, :, pl.ds(DIM, DIM)],
            "value": lambda: s.wqkv.at[layer, :, pl.ds(2 * DIM, DIM)],
            "output": lambda: s.wo.at[layer],
            "second_gain": lambda: s.gain2.at[layer],
            "gate": lambda: s.wg.at[layer],
            "up": lambda: s.wu.at[layer],
            "down": lambda: s.wd.at[layer],
        }
        return where[name]()

    def source(name):
        ref = getattr(s, "in_" + name)
        return ref if name.endswith("gain") else ref.at[0]

    def weight_local(name, layer):
        index = WEIGHTS.index(name)
        return pltpu.make_async_copy(source(name), place(name, layer), s.w_sem.at[layer, index])

    def weight_copy(name, layer):
        index = WEIGHTS.index(name)
        return pltpu.make_async_remote_copy(
            src_ref=source(name),
            dst_ref=place(name, layer),
            send_sem=s.w_send.at[index],
            recv_sem=s.w_sem.at[layer, index],
            device_id=links.to_core,
            device_id_type=MESH,
        )

    def need(layer, *which):
        for name in which:
            weight_local(name, layer).wait()

    for name in WEIGHTS:
        weight_local(name, c).start()

    ids = s.sample_ids[pl.ds(c, 1), :].astype(F32)
    count = [jnp.sum(jnp.where(ids == v, 1.0, 0.0), axis=-1, keepdims=True) for v in range(3)]
    first = jnp.where(
        count[0] == HALF,
        0.0,
        jnp.where(
            count[1] == HALF,
            count[0],
            jnp.where(count[2] == HALF, count[0] + count[1], count[0] + count[1] + count[2]),
        ),
    ).astype(jnp.int32)
    down_iota = lax.broadcasted_iota(jnp.int32, (SEQ, SEQ), 0)
    lane_iota = lax.broadcasted_iota(jnp.int32, (SEQ, SEQ), 1)
    moved = down_iota + first
    moved = jnp.where(moved >= SEQ, moved - SEQ, moved)
    perm = jnp.where(lane_iota == moved, 1.0, 0.0)
    ids_down = jnp.sum(perm[HALF:] * ids, axis=-1, keepdims=True)
    s.perm[...] = perm.astype(BF)
    moved = lane_iota + first
    moved = jnp.where(moved >= SEQ, moved - SEQ, moved)
    s.back[...] = jnp.where(down_iota == moved, 1.0, 0.0).astype(BF)
    ids_lane = mm(jnp.broadcast_to(ids, (16, SEQ)).astype(BF), s.back[:, HALF:])[:1]
    s.mask[...] = jnp.where(ids_down == ids_lane, 0.0, MASKED)

    token_copy.wait()
    s.x[0] = mm(s.perm[...], s.tok[...]).astype(BF)
    cot_copy.wait()
    s.dy[...] = mm(s.perm[...], s.cot[...]).astype(BF)

    links.met()
    for name in WEIGHTS:
        weight_copy(name, c).start()

    head0 = lax.broadcasted_iota(jnp.int32, (HALF, 128), 1) < HEAD_DIM

    def of_head(values, h):
        return jnp.where(head0 if h == 0 else ~head0, values, jnp.zeros_like(values))

    def output_row(layer, src, out, sems):
        @pl.when(layer == c)
        def _():
            pltpu.make_async_copy(src, out.at[c], sems.at[0]).start()

        @pl.when(layer != c)
        def _():
            pltpu.make_async_remote_copy(
                src_ref=src, dst_ref=out.at[c], send_sem=sems.at[1], recv_sem=sems.at[2],
                device_id=links.to_core, device_id_type=MESH,
            ).start()

    def output_settle(src, out, sems):
        pltpu.make_async_copy(src, out.at[c], sems.at[0]).wait()
        pltpu.make_async_remote_copy(
            src_ref=src, dst_ref=out.at[c], send_sem=sems.at[1], recv_sem=sems.at[2],
            device_id=links.to_core, device_id_type=MESH,
        ).wait()

    def forward(layer):
        need(layer, "first_gain", "query", "key", "value")
        x = s.x[layer].astype(F32)
        r = rsqrt_mean(x)
        s.r1[layer] = r
        a = (x * r * s.gain1[layer]).astype(BF)
        s.a[layer] = a
        for lo, hi in ((0, 512), (512, 1024), (1024, 1152)):
            part = mm(a, s.wqkv[layer, :, lo:hi])
            if lo == 0:
                s.qkv[layer, :, :DIM] = (part[:, :DIM] * HEAD_DIM ** (-0.5)).astype(BF)
                s.qkv[layer, :, DIM:hi] = part[:, DIM:].astype(BF)
            else:
                s.qkv[layer, :, lo:hi] = part.astype(BF)

        @pl.loop(0, HEADS // 2)
        def _(pair):
            for block in range(2):
                at = pl.ds(block * HALF, HALF)
                q, k, v = [
                    s.qkv[layer, at, pl.ds(pl.multiple_of(pair * 128 + part * DIM, 128), 128)]
                    for part in range(3)
                ]
                o = None
                for h in range(2):
                    score = mm_nt(q, of_head(k, h))
                    if block == 1:
                        score = score + s.mask[...]
                    expo = jnp.exp(score - jnp.max(score, axis=-1, keepdims=True))
                    total = jnp.sum(expo, axis=-1, keepdims=True)
                    prob = (expo * (1.0 / total)).astype(BF)
                    s.p[layer, pair * 4 + block * 2 + h] = prob
                    term = mm(prob, of_head(v, h))
                    o = term if o is None else o + term
                s.o[layer, at, pl.ds(pl.multiple_of(pair * 128, 128), 128)] = o.astype(BF)

        need(layer, "output", "second_gain")
        x1 = x + mm(s.o[layer], s.wo[layer])
        s.x1[layer] = x1
        r = rsqrt_mean(x1)
        s.r2[layer] = r
        s.b[layer] = (x1 * r * s.gain2[layer]).astype(BF)
        need(layer, "gate", "up", "down")

    def hidden(layer, j):
        at = pl.ds(pl.multiple_of(j * CHUNK, CHUNK), CHUNK)
        b = s.b[layer]
        g = mm(b, s.wg[layer, :, at])
        u = mm(b, s.wu[layer, :, at])
        sig = 1.0 / (1.0 + jnp.exp(-g))
        return at, g, u, sig

    def layer_result(layer, y):
        low = y.astype(BF)
        s.y_row[layer] = mm(s.back[...], low).astype(BF)
        output_row(layer, s.y_row.at[layer], s.rows_out, s.y_sem)
        return low

    @pl.loop(0, 2)
    def _(layer):
        forward(layer)

        @pl.when(layer == 0)
        def _():
            s.acc[...] = s.x1[0]

            @pl.loop(0, 4)
            def _(j):
                at, g, u, sig = hidden(0, j)
                f = (g * sig * u).astype(BF)
                s.acc[...] += mm(f, s.wd[0, at, :])

            s.x[1] = layer_result(0, s.acc[...])

    def put(u, start, values):
        size, width = values.shape
        for lo in range(0, width, 128):
            s.own[u, pl.ds(start, size), :] = values[:, lo : lo + 128].astype(BF)
            start += size
        return start

    def put_gain(layer, which, values):
        for i in range(DIM // 128):
            s.gain_sum[0, pl.ds(layer * 8 + which * 4 + i, 1), :] = values[:, i * 128 : (i + 1) * 128]

    def tick(t, closing=False):
        for step in reversed(range(9)):
            u = t - lag * step
            if closing and step == 0 and lag > 0:
                continue

            @pl.when((u >= 0) & (u < UNITS))
            def _(step=step, u=u):
                links.stage(step, u)

    def made(u):
        links.core_copy(u).start()

    s.gain_sum[0] = jnp.zeros((16, 128), F32)

    @pl.loop(0, 2)
    def _(turn):
        layer = 1 - turn
        base = turn * 6
        s.bt[...] = s.b[layer].T
        s.db[...] = jnp.zeros((SEQ, DIM), F32)

        @pl.when(layer == 1)
        def _():
            s.acc[...] = s.x1[1]

        @pl.loop(0, 4)
        def _(j):
            at, g, u, sig = hidden(layer, j)
            silu = g * sig
            f = (silu * u).astype(BF)
            dy = s.dy[...]
            df = mm_nt(dy, s.wd[layer, at, :])
            dg = (df * u * sig * (1.0 + g * (1.0 - sig))).astype(BF)
            du = (df * silu).astype(BF)
            unit = base + j
            nxt = put(unit, 0, mm_tn(f, dy))
            nxt = put(unit, nxt, mm(s.bt[...], dg))
            put(unit, nxt, mm(s.bt[...], du))
            made(unit)
            s.db[...] += mm_nt(dg, s.wg[layer, :, at]) + mm_nt(du, s.wu[layer, :, at])

            @pl.when(layer == 1)
            def _():
                s.acc[...] += mm(f, s.wd[layer, at, :])

            tick(unit)

        @pl.when(layer == 1)
        def _():
            layer_result(1, s.acc[...])

        db = s.db[...]
        r = s.r2[layer]
        normed = s.x1[layer] * r
        put_gain(layer, 1, jnp.sum(db * normed, axis=0, keepdims=True))
        part = db * s.gain2[layer]
        dx1 = s.dy[...].astype(F32) + r * (part - normed * jnp.mean(part * normed, axis=-1, keepdims=True))
        s.dx1[...] = dx1
        low = dx1.astype(BF)
        nxt = put(base + 4, 0, mm_tn(s.o[layer], low))
        s.do[...] = mm_nt(low, s.wo[layer]).astype(BF)

        @pl.loop(0, HEADS // 2)
        def _(pair):
            for block in range(2):
                at = pl.ds(block * HALF, HALF)
                q, k, v = [
                    s.qkv[layer, at, pl.ds(pl.multiple_of(pair * 128 + part * DIM, 128), 128)]
                    for part in range(3)
                ]
                do = s.do[at, pl.ds(pl.multiple_of(pair * 128, 128), 128)]
                dq = dk = dv = None
                for h in range(2):
                    prob = s.p[layer, pair * 4 + block * 2 + h]
                    tv = mm_tn(prob, of_head(do, h))
                    dp = mm_nt(do, of_head(v, h))
                    wide = prob.astype(F32)
                    ds = (wide * (dp - jnp.sum(wide * dp, axis=-1, keepdims=True))).astype(BF)
                    tq = mm(ds, of_head(k, h))
                    tk = mm_tn(ds, of_head(q, h))
                    dq, dk, dv = (tq, tk, tv) if h == 0 else (dq + tq, dk + tk, dv + tv)
                for part, values in enumerate((dq * HEAD_DIM ** (-0.5), dk, dv)):
                    s.dqkv[at, pl.ds(pl.multiple_of(pair * 128 + part * DIM, 128), 128)] = values.astype(BF)

        s.at[...] = s.a[layer].T
        put(base + 4, nxt, mm(s.at[...], s.dqkv[:, :DIM]))
        made(base + 4)
        tick(base + 4)
        nxt = put(base + 5, 0, mm(s.at[...], s.dqkv[:, DIM : 2 * DIM]))
        put(base + 5, nxt, mm(s.at[...], s.dqkv[:, 2 * DIM :]))
        made(base + 5)

        da = mm_nt(s.dqkv[...], s.wqkv[layer])
        r = s.r1[layer]
        normed = s.x[layer].astype(F32) * r
        put_gain(layer, 0, jnp.sum(da * normed, axis=0, keepdims=True))
        part = da * s.gain1[layer]
        dx = s.dx1[...] + r * (part - normed * jnp.mean(part * normed, axis=-1, keepdims=True))
        low = dx.astype(BF)
        s.dy[...] = low
        s.dx_row[layer] = mm(s.back[...], low).astype(BF)
        output_row(layer, s.dx_row.at[layer], s.dx_out, s.dx_sem)
        tick(base + 5)

    links.sum_gains()

    @pl.loop(UNITS, UNITS + 8 * lag)
    def _(t):
        tick(t, closing=True)

    s.gains_out[...] = s.gain_sum[6, pl.ds(pl.multiple_of(c * 8, 8), 8), :]

    @pl.loop(0, UNITS)
    def _(u):
        links.settle(u)

    for index, name in enumerate(WEIGHTS):
        weight_copy(name, c).wait_send()
    output_settle(s.y_row.at[0], s.rows_out, s.y_sem)
    output_settle(s.dx_row.at[0], s.dx_out, s.dx_sem)


def spread_kernel(units, rows_in, dx_in, gains_in, rows_out, dx_out, *outs):
    first, query, key, value, output, second, gate, up, down = outs
    i = pl.program_id(0)

    @pl.when(i < 4)
    def _():
        for p in range(3):
            down[0, :, p * 128 : (p + 1) * 128] = units[0, pl.ds(p * CHUNK, CHUNK), :].astype(F32)
        for p in range(2):
            gate[0, :, p * 128 : (p + 1) * 128] = units[0, pl.ds((2 + p) * DIM, DIM), :].astype(F32)
            up[0, :, p * 128 : (p + 1) * 128] = units[0, pl.ds((4 + p) * DIM, DIM), :].astype(F32)
        rows_out[0] = rows_in[...]
        dx_out[0] = dx_in[...].astype(F32)

    def square(ref, panel):
        for p in range(3):
            ref[0, :, p * 128 : (p + 1) * 128] = units[0, pl.ds((panel + p) * DIM, DIM), :].astype(F32)

    @pl.when(i == 4)
    def _():
        square(output, 0)
        square(query, 3)

    @pl.when(i == 5)
    def _():
        square(key, 0)
        square(value, 3)
        for p in range(3):
            first[:, p * 128 : (p + 1) * 128] = gains_in[p : p + 1, :]
            second[:, p * 128 : (p + 1) * 128] = gains_in[4 + p : 5 + p, :]


def spread(units, rows_in, dx_in, gains):
    part = lambda i: jnp.minimum(i, 3)
    whole3 = pl.BlockSpec((1, DIM, DIM), lambda i: (0, 0, 0))
    vector = pl.BlockSpec((1, DIM), lambda i: (0, 0))
    row_block = lambda: pl.BlockSpec((1, 1, HALF, DIM), lambda i: (0, part(i) // 2, part(i) % 2, 0))
    row_in = lambda: pl.BlockSpec((1, HALF, DIM), lambda i: (part(i) // 2, part(i) % 2, 0))
    wide = lambda: pl.BlockSpec((1, DIM, CHUNK), lambda i: (0, 0, part(i)))
    square = jax.ShapeDtypeStruct((1, DIM, DIM), F32)
    return pl.pallas_call(
        spread_kernel,
        grid=(6,),
        in_specs=[
            pl.BlockSpec((1, UNIT, 128), lambda i: (i, 0, 0)),
            row_in(),
            row_in(),
            pl.BlockSpec((8, 128), lambda i: (0, 0)),
        ],
        out_specs=[
            row_block(), row_block(), vector, whole3, whole3, whole3, whole3, vector, wide(), wide(),
            pl.BlockSpec((1, CHUNK, DIM), lambda i: (0, part(i), 0)),
        ],
        out_shape=[
            jax.ShapeDtypeStruct((1, 2, SEQ, DIM), BF),
            jax.ShapeDtypeStruct((1, 2, SEQ, DIM), F32),
            jax.ShapeDtypeStruct((1, DIM), F32),
            square, square, square, square,
            jax.ShapeDtypeStruct((1, DIM), F32),
            jax.ShapeDtypeStruct((1, DIM, FF), F32),
            jax.ShapeDtypeStruct((1, DIM, FF), F32),
            jax.ShapeDtypeStruct((1, FF, DIM), F32),
        ],
        compiler_params=pltpu.CompilerParams(vmem_limit_bytes=32 * 2**20),
    )(units, rows_in, dx_in, gains)


def layers(lag, tokens, sample_ids, cotangent, *weights):
    anywhere = pl.BlockSpec(memory_space=pl.ANY)
    vmem = pl.BlockSpec(memory_space=pltpu.VMEM)
    inputs = ["tokens", "cotangent"] + ["in_" + name for name in WEIGHTS] + ["sample_ids"]
    outputs = {
        "grads_out": jax.ShapeDtypeStruct((UNITS // 2, UNIT, 128), BF),
        "rows_out": jax.ShapeDtypeStruct((2, SEQ, DIM), BF),
        "dx_out": jax.ShapeDtypeStruct((2, SEQ, DIM), BF),
        "gains_out": jax.ShapeDtypeStruct((8, 128), F32),
    }
    dma = pltpu.SemaphoreType.DMA
    scratch = {
        "tok": pltpu.VMEM((SEQ, DIM), BF),
        "cot": pltpu.VMEM((SEQ, DIM), BF),
        "gain1": pltpu.VMEM((2, 1, DIM), F32),
        "gain2": pltpu.VMEM((2, 1, DIM), F32),
        "wqkv": pltpu.VMEM((2, DIM, 3 * DIM), BF),
        "wo": pltpu.VMEM((2, DIM, DIM), BF),
        "wg": pltpu.VMEM((2, DIM, FF), BF),
        "wu": pltpu.VMEM((2, DIM, FF), BF),
        "wd": pltpu.VMEM((2, FF, DIM), BF),
        "perm": pltpu.VMEM((SEQ, SEQ), BF),
        "back": pltpu.VMEM((SEQ, SEQ), BF),
        "mask": pltpu.VMEM((HALF, HALF), F32),
        "x": pltpu.VMEM((2, SEQ, DIM), BF),
        "a": pltpu.VMEM((2, SEQ, DIM), BF),
        "qkv": pltpu.VMEM((2, SEQ, 3 * DIM), BF),
        "p": pltpu.VMEM((2, 2 * HEADS, HALF, HALF), BF),
        "o": pltpu.VMEM((2, SEQ, DIM), BF),
        "x1": pltpu.VMEM((2, SEQ, DIM), F32),
        "b": pltpu.VMEM((2, SEQ, DIM), BF),
        "r1": pltpu.VMEM((2, SEQ, 1), F32),
        "r2": pltpu.VMEM((2, SEQ, 1), F32),
        "acc": pltpu.VMEM((SEQ, DIM), F32),
        "bt": pltpu.VMEM((DIM, SEQ), BF),
        "at": pltpu.VMEM((DIM, SEQ), BF),
        "db": pltpu.VMEM((SEQ, DIM), F32),
        "dy": pltpu.VMEM((SEQ, DIM), BF),
        "dx1": pltpu.VMEM((SEQ, DIM), F32),
        "do": pltpu.VMEM((SEQ, DIM), BF),
        "dqkv": pltpu.VMEM((SEQ, 3 * DIM), BF),
        "y_row": pltpu.VMEM((2, SEQ, DIM), BF),
        "dx_row": pltpu.VMEM((2, SEQ, DIM), BF),
        "own": pltpu.VMEM((UNITS, UNIT, 128), BF),
        "part": pltpu.VMEM((UNITS, SHARE, 128), BF),
        "land": pltpu.VMEM((UNITS, LAND_ROWS, 128), BF),
        "done": pltpu.VMEM((UNITS, SHARE, 128), BF),
        "gain_sum": pltpu.VMEM((7, 16, 128), F32),
        "gain_land": pltpu.VMEM((6, 16, 128), F32),
        "in_sem": dma((2,)),
        "w_sem": dma((2, len(WEIGHTS))),
        "w_send": dma((len(WEIGHTS),)),
        "send": dma((UNITS, len(COPIES))),
        "recv": dma((UNITS, len(COPIES))),
        "gain_send": dma((6,)),
        "gain_recv": dma((6,)),
        "y_sem": dma((3,)),
        "dx_sem": dma((3,)),
    }
    names = inputs + list(outputs) + list(scratch)
    return pl.pallas_call(
        functools.partial(kernel, names, lag),
        out_shape=list(outputs.values()),
        in_specs=[anywhere] * (len(inputs) - 1) + [vmem],
        out_specs=[anywhere, anywhere, anywhere, vmem],
        scratch_shapes=list(scratch.values()),
        compiler_params=pltpu.CompilerParams(
            collective_id=0, has_side_effects=True, vmem_limit_bytes=62 * 2**20
        ),
        cost_estimate=pl.CostEstimate(flops=15 * 10**9, bytes_accessed=10**7, transcendentals=4 * 10**6),
    )(tokens, cotangent, *weights, sample_ids)


def solution(mesh):
    count = mesh.shape["dp"]

    def per_device(tokens, sample_ids, cotangent, *weights):
        units, rows_out, dx_out, gains = layers(2, tokens, sample_ids, cotangent, *weights)
        outs = spread(units, rows_out, dx_out, gains)
        if count > GROUP:
            members = [[g * GROUP + i for g in range(count // GROUP)] for i in range(GROUP)]
            outs = list(outs[:2]) + list(lax.psum(tuple(outs[2:]), "dp", axis_index_groups=members))
        return tuple(outs)

    matrix = P("section", None, None)
    vector = P("section", None)
    rows4 = P("section", "dp", None, None)
    grads = (vector, matrix, matrix, matrix, matrix, vector, matrix, matrix, matrix)
    return jax.shard_map(
        per_device,
        mesh=mesh,
        in_specs=(P("dp", None, None), P("dp", None), P("dp", None, None)) + grads,
        out_specs=(rows4, rows4) + grads,
        check_vma=False,
    )
```

time: 445 us -> 127 us (0.29); the launches traced: 439 us -> 127 us
  matrix products: 162 us -> 0 us
  waiting for transfers between devices: 153 us -> 0 us
  Pallas kernels: 0 us -> 121 us
  blocking collectives: 44.9 us -> 0 us
  other arithmetic: 29.5 us -> 0 us
  local copies, waits for them, and re-layouts: 25.5 us -> 4.94 us
  between operations: 16.4 us -> 0.67 us
  starting transfers between devices: 8.36 us -> 0 us
    psum x1 -> x0, waiting for transfers between devices: 153 us -> none  [final_total(): lax.psum((grad_first, grad_query, grad_key, grad_value, grad_output, grad...]
    dot_general x99 -> x0, matrix products: 144 us -> none  [the longest x36 52.9 us: matmul(): return jnp.dot(left, right, preferred_element_type=jnp.float32)]
    pallas_call x0 -> x2, Pallas kernels: none -> 121 us  [the longest x1 117 us: layers(): pl.pallas_call(functools.partial(kernel, names, lag), out_shape=list(outp...]
    psum x1 -> x0, blocking collectives: 44.9 us -> none  [final_total(): lax.psum((grad_first, grad_query, grad_key, grad_value, grad_output, grad...]
    sub x3 -> x0, matrix products: 17.8 us -> none  [attend_row(): expo = jnp.exp(scores - top_score)]
    unnamed x277 -> x8, local copies, waits for them, and re-layouts: 22.4 us -> 4.94 us
    convert_element_type x5 -> x0, other arithmetic: 12.2 us -> none  [the longest x3 11.1 us: attend_back(): grad_scores = (probs * (grad_probs - jnp.sum(probs * grad_probs, axis=-1,...]
    ppermute x4 -> x0, starting transfers between devices: 8.33 us -> none  [shifted(): return lax.ppermute(block, axis, route)]
  transfers between devices with their start and end apart: 5 -> 0, of which waited for: 1 -> 0; matrix products, arithmetic and copies ran while one was open for 14% -> 0% of each run, Pallas kernels for 0% -> 0%
where the time goes in v1:
time: 127 us
  Pallas kernels  121 us (95%)
  local copies, waits for them, and re-layouts  4.94 us (4%)
    pallas_call x1, Pallas kernels, layers(): pl.pallas_call(functools.partial(kernel, names, lag), out_shape=list(outp...  117 us
    unnamed x8, local copies, waits for them, and re-layouts  4.94 us
    pallas_call x1, Pallas kernels, spread(): pl.pallas_call(spread_kernel, grid=(6,), in_specs=[pl.BlockSpec((1, UNIT,...  4.88 us

profile of v1, /device:TPU:0, one launch (start us, length us, event | category | flops | bytes accessed | tf_op | source)
XLA Modules:
  0.0 127.1 jit_solution(1306140527124778135)
XLA Ops:
  0.6 116.6 %shard_map.203 = (bf16[6,2304,128]{2,1,0:T(8,128)(2,1)}, bf16[2,512,384]{2,1,0:T(8,128)(2,1)}, bf16[2,512,384]{2,1,0:T(8,128)(2,1)}, f32[8,128]{1,0:T(8,128)}) custom-call(bf16[2,512,384]{2,1,0:T(8,128)(2,1)} %refs_0_.1, bf16[2,512,384]{2,1,0:T(8,128)(2,1)} %refs_1_.1, f32[1,384]{1,0:T(1,128)} %refs_2_.1, bf16[1,384,384]{2,1,0:T(8,128)(2,1)} %refs_3_.1, ...), custom_call_target="tpu_custom_call" | custom-call | flops 15000000512 | bytes 10000000 | tf_op jit(solution)/shard_map/pallas_call | solution.py:803
  117.3 0.0 copy-start
  117.3 2.0 %copy-done = bf16[6,2304,128]{2,1,0:T(8,128)(2,1)S(1)} copy-done((bf16[6,2304,128]{2,1,0:T(8,128)(2,1)S(1)}, bf16[6,2304,128]{2,1,0:T(8,128)(2,1)}, u32[]{:S(2)}) %copy-start) | copy-done | bytes 3538968
  119.3 0.0 copy-start.1
  119.3 1.1 copy-done.1
  120.4 0.0 copy-start.2
  120.4 1.1 copy-done.2
  121.5 0.0 copy-start.3
  121.5 0.7 copy-done.3
  122.2 4.9 %shard_map.204 = (bf16[1,2,512,384]{3,2,1,0:T(8,128)(2,1)}, f32[1,2,512,384]{3,2,1,0:T(8,128)}, f32[1,384]{1,0:T(1,128)}, f32[1,384,384]{2,1,0:T(8,128)}, f32[1,...) custom-call(bf16[6,2304,128]{2,1,0:T(8,128)(2,1)S(1)} %copy-done, ...), custom_call_target="tpu_custom_call" | custom-call | tf_op jit(solution)/shard_map/pallas_call | solution.py:716
Async XLA Ops:
  117.3 2.0 %copy-start = (bf16[6,2304,128]{2,1,0:T(8,128)(2,1)S(1)}, bf16[6,2304,128]{2,1,0:T(8,128)(2,1)}, u32[]{:S(2)}) copy-start(bf16[6,2304,128]{2,1,0:T(8,128)(2,1)} %get-tuple-element.15.units) | copy-start | bytes 10616836
  119.3 1.1 copy-start.1
  120.4 1.1 copy-start.2
  121.5 0.7 copy-start.3

commit v2 on v1

--- a/solution.py
+++ b/solution.py
@@ -25,22 +25,12 @@
 UNITS = 12
 UNIT = 2304
 SHARE = UNIT // 2
-PA = 384
-PC = SHARE - 2 * PA
-
-LANDINGS = (
-    ("A1", PA // 2), ("A2", PA // 4), ("A3", PA // 4), ("A4", PA // 8),
-    ("B1", PA // 2), ("B2", PA // 4), ("B3", PA // 4), ("B4", PA // 8),
-    ("C1", PC), ("C2", PC // 2), ("C3", PC // 4), ("C4", PC // 8),
-)
-LAND = {}
-LAND_ROWS = 0
-for _name, _rows in LANDINGS:
-    LAND[_name] = (LAND_ROWS, _rows)
-    LAND_ROWS += _rows
-
-COPIES = ["K"] + [part + str(step) for part in "ABC" for step in range(1, 9)] + ["F"]
-SEM = {name: index for index, name in enumerate(COPIES)}
+PIECE = SHARE // 3
+SIZES = (PIECE // 2, PIECE // 4, PIECE // 8)
+LAND_AT = (0, PIECE // 2, 3 * PIECE // 4, 7 * PIECE // 8)
+STAGES = 8
+
+SENT = 3 * sum(SIZES) * 2 + 3 * SIZES[2]
 
 
 def mm(a, b):
@@ -69,83 +59,81 @@
         self.c = lax.axis_index("section")
         self.dp = lax.axis_index("dp")
         local = lax.rem(self.dp, GROUP)
-        self.x = lax.rem(local, 2)
-        self.y = lax.rem(lax.div(local, 2), 2)
-        self.z = lax.div(local, 4)
-        self.middle = (self.z == 1) | (self.z == 2)
-        self.end = (self.z == 0) | (self.z == 3)
-        self.m = lax.div(self.z, 2)
-        self.to_core = (1 - self.c, self.dp)
-        self.to_x = (self.c, self.dp + 1 - 2 * self.x)
-        self.to_y = (self.c, self.dp + 2 - 4 * self.y)
-        self.to_pair = (self.c, self.dp + 4 - 8 * lax.rem(self.z, 2))
-        self.to_middle = (self.c, self.dp + 4 - 8 * self.m)
-        self.a1 = self.x * (PA // 2)
-        self.a2 = self.a1 + self.y * (PA // 4)
-        self.a3 = self.a2 + self.m * (PA // 8)
-        self.b1 = PA + self.y * (PA // 2)
-        self.b2 = self.b1 + self.x * (PA // 4)
-        self.b3 = self.b2 + self.m * (PA // 8)
-        self.c0 = 2 * PA
-        self.c1 = self.c0 + self.m * (PC // 2)
-        self.c2 = self.c1 + self.x * (PC // 4)
-        self.c3 = self.c2 + self.y * (PC // 8)
+        x = lax.rem(local, 2)
+        y = lax.rem(lax.div(local, 2), 2)
+        p = lax.rem(lax.div(local, 4), 2)
+        q = lax.div(local, 8)
+        c = self.c
+        self.to_core = (1 - c, self.dp)
+        step_x, step_y = 1 - 2 * x, 2 - 4 * y
+        self.to_x = (c, self.dp + step_x)
+        self.to_y = (c, self.dp + step_y)
+        self.to_p = (c, self.dp + 4 - 8 * p)
+        self.to_q = (c, self.dp + 8 - 16 * q)
+        along_x, along_y, along_p = (x, self.to_x), (y, self.to_y), (p, self.to_p)
+        one = (x + c * (y - x), (c, self.dp + step_x + c * (step_y - step_x)))
+        two = (y + c * (x - y), (c, self.dp + step_y + c * (step_x - step_y)))
+        orders = ((along_x, along_y, along_p), (along_y, along_x, along_p), (along_p, one, two))
+        self.pieces = []
+        for index, order in enumerate(orders):
+            starts = [index * PIECE]
+            for (bit, _), size in zip(order, SIZES):
+                starts.append(starts[-1] + bit * size)
+            self.pieces.append((index, order, starts))
 
     def meet(self):
         barrier = pltpu.get_barrier_semaphore()
-        for target in (self.to_core, self.to_x, self.to_y, self.to_pair):
+        for target in (self.to_core, self.to_x, self.to_y, self.to_p, self.to_q):
             pl.semaphore_signal(barrier, inc=1, device_id=target, device_id_type=MESH)
 
-        @pl.when(self.middle)
-        def _():
-            pl.semaphore_signal(barrier, inc=1, device_id=self.to_middle, device_id_type=MESH)
-
     def met(self):
-        barrier = pltpu.get_barrier_semaphore()
-
-        @pl.when(self.middle)
-        def _():
-            pl.semaphore_wait(barrier, 5)
-
-        @pl.when(self.end)
-        def _():
-            pl.semaphore_wait(barrier, 4)
-
-    def copy(self, u, name, src, dst, target):
+        pl.semaphore_wait(pltpu.get_barrier_semaphore(), 5)
+
+    def copy(self, u, step, src, dst, target):
         return pltpu.make_async_remote_copy(
             src_ref=src,
             dst_ref=dst,
-            send_sem=self.s.send.at[u, SEM[name]],
-            recv_sem=self.s.recv.at[u, SEM[name]],
+            send_sem=self.s.sent.at[u],
+            recv_sem=self.s.recv.at[u, step],
             device_id=target,
             device_id_type=MESH,
         )
 
-    def down(self, u, name, start, target):
-        place, size = LAND[name]
-        return self.copy(
-            u, name, self.s.part.at[u, rows(start, size)], self.s.land.at[u, rows(place, size)], target
-        )
-
-    def up(self, u, name, start, size, target):
-        here = self.s.done.at[u, rows(start, size)]
-        return self.copy(u, name, here, here, target)
-
-    def arrived(self, u, name, start):
-        place, size = LAND[name]
-        self.down(u, name, start, self.to_core).wait_recv()
-        here = rows(start, size)
-        self.s.part[u, here] = self.s.part[u, here] + self.s.land[u, rows(place, size)]
-
-    def finish(self, u, name, start):
-        place, size = LAND[name]
-        self.down(u, name, start, self.to_core).wait_recv()
-        here = rows(start, size)
-        self.s.done[u, here] = self.s.part[u, here] + self.s.land[u, rows(place, size)]
+    def landing(self, index, step):
+        size = SIZES[min(step, 2)]
+        return pl.ds(index * PIECE + LAND_AT[step], size)
+
+    def piece_copy(self, u, piece, step):
+        index, order, starts = piece
+        s = self.s
+        if step < 3:
+            (bit, target), size = order[step], SIZES[step]
+            src = s.part.at[u, rows(starts[step] + (1 - bit) * size, size)]
+            return self.copy(u, step, src, s.land.at[u, self.landing(index, step)], target)
+        if step == 3:
+            src = s.part.at[u, rows(starts[3], SIZES[2])]
+            return self.copy(u, 3, src, s.land.at[u, self.landing(index, 3)], self.to_q)
+        back = 6 - step
+        here = s.done.at[u, rows(starts[back + 1], SIZES[back])]
+        return self.copy(u, step, here, here, order[back][1])
+
+    def arrived(self, u, step):
+        size = 3 * SIZES[(0, 1, 2, 2, 2, 1, 0)[step]]
+        there = self.s.land.at[u, pl.ds(0, size)]
+        self.copy(u, step, there, there, self.to_core).wait_recv()
+
+    def all_sent(self, u):
+        here = self.s.own.at[u, pl.ds(0, SENT)]
+        self.copy(u, 0, here, here, self.to_core).wait_send()
 
     def core_copy(self, u):
-        return self.copy(
-            u, "K", self.s.own.at[u, rows((1 - self.c) * SHARE, SHARE)], self.s.part.at[u], self.to_core
+        return pltpu.make_async_remote_copy(
+            src_ref=self.s.own.at[u, rows((1 - self.c) * SHARE, SHARE)],
+            dst_ref=self.s.part.at[u],
+            send_sem=self.s.core_sent.at[u],
+            recv_sem=self.s.core_recv.at[u],
+            device_id=self.to_core,
+            device_id_type=MESH,
         )
 
     def result(self, u):
@@ -153,147 +141,44 @@
         return self.s.grads_out.at[place, rows(self.c * SHARE, SHARE)]
 
     def result_local(self, u):
-        return pltpu.make_async_copy(self.s.done.at[u], self.result(u), self.s.send.at[u, SEM["F"]])
+        return pltpu.make_async_copy(self.s.done.at[u], self.result(u), self.s.out_sent.at[u])
 
     def result_copy(self, u):
-        return self.copy(u, "F", self.s.done.at[u], self.result(u), self.to_core)
-
-    def sends(self):
-        every, middle, end = None, self.middle, self.end
-        return {
-            "A1": (lambda u: self.down(u, "A1", (1 - self.x) * (PA // 2), self.to_x), every),
-            "A2": (lambda u: self.down(u, "A2", self.a1 + (1 - self.y) * (PA // 4), self.to_y), every),
-            "A3": (lambda u: self.down(u, "A3", self.a2, self.to_pair), end),
-            "A4": (lambda u: self.down(u, "A4", self.a2 + (1 - self.m) * (PA // 8), self.to_middle), middle),
-            "A5": (lambda u: self.up(u, "A5", self.a3, PA // 8, self.to_middle), middle),
-            "A6": (lambda u: self.up(u, "A6", self.a2, PA // 4, self.to_pair), middle),
-            "A7": (lambda u: self.up(u, "A7", self.a2, PA // 4, self.to_y), every),
-            "A8": (lambda u: self.up(u, "A8", self.a1, PA // 2, self.to_x), every),
-            "B1": (lambda u: self.down(u, "B1", PA + (1 - self.y) * (PA // 2), self.to_y), every),
-            "B2": (lambda u: self.down(u, "B2", self.b1 + (1 - self.x) * (PA // 4), self.to_x), every),
-            "B3": (lambda u: self.down(u, "B3", self.b2, self.to_pair), end),
-            "B4": (lambda u: self.down(u, "B4", self.b2 + (1 - self.m) * (PA // 8), self.to_middle), middle),
-            "B5": (lambda u: self.up(u, "B5", self.b3, PA // 8, self.to_middle), middle),
-            "B6": (lambda u: self.up(u, "B6", self.b2, PA // 4, self.to_pair), middle),
-            "B7": (lambda u: self.up(u, "B7", self.b2, PA // 4, self.to_x), every),
-            "B8": (lambda u: self.up(u, "B8", self.b1, PA // 2, self.to_y), every),
-            "C1": (lambda u: self.down(u, "C1", self.c0, self.to_pair), end),
-            "C2": (lambda u: self.down(u, "C2", self.c0 + (1 - self.m) * (PC // 2), self.to_middle), middle),
-            "C3": (lambda u: self.down(u, "C3", self.c1 + (1 - self.x) * (PC // 4), self.to_x), middle),
-            "C4": (lambda u: self.down(u, "C4", self.c2 + (1 - self.y) * (PC // 8), self.to_y), middle),
-            "C5": (lambda u: self.up(u, "C5", self.c3, PC // 8, self.to_y), middle),
-            "C6": (lambda u: self.up(u, "C6", self.c2, PC // 4, self.to_x), middle),
-            "C7": (lambda u: self.up(u, "C7", self.c1, PC // 2, self.to_middle), middle),
-            "C8": (lambda u: self.up(u, "C8", self.c0, PC, self.to_pair), middle),
-        }
+        return pltpu.make_async_remote_copy(
+            src_ref=self.s.done.at[u],
+            dst_ref=self.result(u),
+            send_sem=self.s.out_sent.at[u],
+            recv_sem=self.s.out_recv.at[u],
+            device_id=self.to_core,
+            device_id_type=MESH,
+        )
 
     def stage(self, step, u):
-        table = self.sends()
-
-        def start(*names):
-            for name in names:
-                table[name][0](u).start()
-
-        def landed(name, size, at):
-            self.up(u, name, at, size, self.to_core).wait_recv()
-
+        s = self.s
         if step == 0:
             self.core_copy(u).wait_recv()
-            mine = rows(self.c * SHARE, SHARE)
-            self.s.part[u] = self.s.part[u] + self.s.own[u, mine]
-            start("A1", "B1")
-            pl.when(self.end)(lambda: start("C1"))
-        elif step == 1:
-            self.arrived(u, "A1", self.a1)
-            start("A2")
-            self.arrived(u, "B1", self.b1)
-            start("B2")
-
-            @pl.when(self.middle)
-            def _():
-                self.arrived(u, "C1", self.c0)
-                start("C2")
-        elif step == 2:
-            self.arrived(u, "A2", self.a2)
-            self.arrived(u, "B2", self.b2)
-            pl.when(self.end)(lambda: start("A3", "B3"))
-
-            @pl.when(self.middle)
-            def _():
-                self.arrived(u, "C2", self.c1)
-                start("C3")
-        elif step == 3:
-
-            @pl.when(self.middle)
-            def _():
-                self.arrived(u, "A3", self.a2)
-                start("A4")
-                self.arrived(u, "B3", self.b2)
-                start("B4")
-                self.arrived(u, "C3", self.c2)
-                start("C4")
-        elif step == 4:
-
-            @pl.when(self.middle)
-            def _():
-                self.finish(u, "A4", self.a3)
-                start("A5")
-                self.finish(u, "B4", self.b3)
-                start("B5")
-                self.finish(u, "C4", self.c3)
-                start("C5")
-        elif step == 5:
-
-            @pl.when(self.middle)
-            def _():
-                landed("A5", PA // 8, self.a3)
-                start("A6", "A7")
-                landed("B5", PA // 8, self.b3)
-                start("B6", "B7")
-                landed("C5", PC // 8, self.c3)
-                start("C6")
-        elif step == 6:
-
-            @pl.when(self.end)
-            def _():
-                landed("A6", PA // 4, self.a2)
-                start("A7")
-                landed("B6", PA // 4, self.b2)
-                start("B7")
-
-            @pl.when(self.middle)
-            def _():
-                landed("C6", PC // 4, self.c2)
-                start("C7")
-        elif step == 7:
-            landed("A7", PA // 4, self.a2)
-            start("A8")
-            landed("B7", PA // 4, self.b2)
-            start("B8")
-
-            @pl.when(self.middle)
-            def _():
-                landed("C7", PC // 2, self.c1)
-                start("C8")
-        elif step == 8:
-            landed("A8", PA // 2, self.a1)
-            landed("B8", PA // 2, self.b1)
-
-            @pl.when(self.end)
-            def _():
-                landed("C8", PC, self.c0)
-
+            s.part[u] = s.part[u] + s.own[u, rows(self.c * SHARE, SHARE)]
+        else:
+            self.arrived(u, step - 1)
+        for piece in self.pieces:
+            index, _, starts = piece
+            if 1 <= step <= 4:
+                here = rows(starts[min(step, 3)], SIZES[min(step - 1, 2)])
+                total = s.part[u, here] + s.land[u, self.landing(index, step - 1)]
+                if step < 4:
+                    s.part[u, here] = total
+                else:
+                    s.done[u, here] = total
+            if step < 7:
+                self.piece_copy(u, piece, step).start()
+        if step == 7:
             layer = 1 - lax.div(u, 6)
             pl.when(layer == self.c)(lambda: self.result_local(u).start())
             pl.when(layer != self.c)(lambda: self.result_copy(u).start())
+            self.core_copy(u).wait_send()
+            self.all_sent(u)
 
     def settle(self, u):
-        self.core_copy(u).wait_send()
-        for make, who in self.sends().values():
-            if who is None:
-                make(u).wait_send()
-            else:
-                pl.when(who)(lambda make=make: make(u).wait_send())
         layer = 1 - lax.div(u, 6)
 
         @pl.when(layer == self.c)
@@ -305,53 +190,26 @@
         def _():
             self.result_copy(u).wait_send()
 
-    def sum_gains(self):
+    def sum_gains(self, step):
         s = self.s
         total = s.gain_sum
-
-        def copy(index, target):
+        targets = (self.to_core, self.to_x, self.to_y, self.to_p, self.to_q)
+
+        def copy(index):
             return pltpu.make_async_remote_copy(
                 src_ref=total.at[index],
                 dst_ref=s.gain_land.at[index],
                 send_sem=s.gain_send.at[index],
                 recv_sem=s.gain_recv.at[index],
-                device_id=target,
+                device_id=targets[index],
                 device_id_type=MESH,
             )
 
-        for index, target in enumerate((self.to_core, self.to_x, self.to_y)):
-            one = copy(index, target)
-            one.start()
-            one.wait_recv()
-            total[index + 1] = total[index] + s.gain_land[index]
-
-        @pl.when(self.end)
-        def _():
-            copy(3, self.to_pair).start()
-            copy(5, self.to_pair).wait_recv()
-            total[6] = s.gain_land[5]
-
-        @pl.when(self.middle)
-        def _():
-            copy(3, self.to_pair).wait_recv()
-            total[4] = total[3] + s.gain_land[3]
-            copy(4, self.to_middle).start()
-            copy(4, self.to_middle).wait_recv()
-            total[5] = total[4] + s.gain_land[4]
-            copy(5, self.to_pair).start()
-            total[6] = total[5]
-
-        for index in range(3):
-            copy(index, self.to_core).wait_send()
-
-        @pl.when(self.end)
-        def _():
-            copy(3, self.to_pair).wait_send()
-
-        @pl.when(self.middle)
-        def _():
-            copy(4, self.to_middle).wait_send()
-            copy(5, self.to_pair).wait_send()
+        if step > 0:
+            copy(step - 1).wait()
+            total[step] = total[step - 1] + s.gain_land[step - 1]
+        if step < 5:
+            copy(step).start()
 
 
 WEIGHTS = ("first_gain", "query", "key", "value", "output", "second_gain", "gate", "up", "down")
@@ -550,13 +408,14 @@
         for i in range(DIM // 128):
             s.gain_sum[0, pl.ds(layer * 8 + which * 4 + i, 1), :] = values[:, i * 128 : (i + 1) * 128]
 
-    def tick(t, closing=False):
-        for step in reversed(range(9)):
-            u = t - lag * step
-            if closing and step == 0 and lag > 0:
+    def tick(t, odd):
+        for step in reversed(range(STAGES)):
+            wait = 2 + lag * step
+            if wait % 2 != odd:
                 continue
-
-            @pl.when((u >= 0) & (u < UNITS))
+            u = lax.div(2 * t + odd - wait, 2)
+
+            @pl.when((2 * t + odd >= wait) & (u < UNITS))
             def _(step=step, u=u):
                 links.stage(step, u)
 
@@ -586,6 +445,7 @@
             dg = (df * u * sig * (1.0 + g * (1.0 - sig))).astype(BF)
             du = (df * silu).astype(BF)
             unit = base + j
+            tick(unit, 0)
             nxt = put(unit, 0, mm_tn(f, dy))
             nxt = put(unit, nxt, mm(s.bt[...], dg))
             put(unit, nxt, mm(s.bt[...], du))
@@ -596,7 +456,7 @@
             def _():
                 s.acc[...] += mm(f, s.wd[layer, at, :])
 
-            tick(unit)
+            tick(unit, 1)
 
         @pl.when(layer == 1)
         def _():
@@ -637,10 +497,12 @@
 
         s.at[...] = s.a[layer].T
         put(base + 4, nxt, mm(s.at[...], s.dqkv[:, :DIM]))
+        tick(base + 4, 0)
         made(base + 4)
-        tick(base + 4)
+        tick(base + 4, 1)
         nxt = put(base + 5, 0, mm(s.at[...], s.dqkv[:, DIM : 2 * DIM]))
         put(base + 5, nxt, mm(s.at[...], s.dqkv[:, 2 * DIM :]))
+        tick(base + 5, 0)
         made(base + 5)
 
         da = mm_nt(s.dqkv[...], s.wqkv[layer])
@@ -653,15 +515,21 @@
         s.dy[...] = low
         s.dx_row[layer] = mm(s.back[...], low).astype(BF)
         output_row(layer, s.dx_row.at[layer], s.dx_out, s.dx_sem)
-        tick(base + 5)
-
-    links.sum_gains()
-
-    @pl.loop(UNITS, UNITS + 8 * lag)
+        tick(base + 5, 1)
+
+    last = 2 * (UNITS - 1) + 2 + lag * (STAGES - 1)
+
+    @pl.loop(UNITS, max(last // 2, UNITS + 10) + 1)
     def _(t):
-        tick(t, closing=True)
-
-    s.gains_out[...] = s.gain_sum[6, pl.ds(pl.multiple_of(c * 8, 8), 8), :]
+        for odd in range(2):
+            tick(t, odd)
+        for step in range(6):
+
+            @pl.when(t == UNITS + 2 * step)
+            def _(step=step):
+                links.sum_gains(step)
+
+    s.gains_out[...] = s.gain_sum[5, pl.ds(pl.multiple_of(c * 8, 8), 8), :]
 
     @pl.loop(0, UNITS)
     def _(u):
@@ -736,7 +604,7 @@
             jax.ShapeDtypeStruct((1, DIM, FF), F32),
             jax.ShapeDtypeStruct((1, FF, DIM), F32),
         ],
-        compiler_params=pltpu.CompilerParams(vmem_limit_bytes=32 * 2**20),
+        compiler_params=pltpu.CompilerParams(vmem_limit_bytes=62 * 2**20),
     )(units, rows_in, dx_in, gains)
 
 
@@ -785,17 +653,21 @@
         "dx_row": pltpu.VMEM((2, SEQ, DIM), BF),
         "own": pltpu.VMEM((UNITS, UNIT, 128), BF),
         "part": pltpu.VMEM((UNITS, SHARE, 128), BF),
-        "land": pltpu.VMEM((UNITS, LAND_ROWS, 128), BF),
+        "land": pltpu.VMEM((UNITS, SHARE, 128), BF),
         "done": pltpu.VMEM((UNITS, SHARE, 128), BF),
-        "gain_sum": pltpu.VMEM((7, 16, 128), F32),
-        "gain_land": pltpu.VMEM((6, 16, 128), F32),
+        "gain_sum": pltpu.VMEM((6, 16, 128), F32),
+        "gain_land": pltpu.VMEM((5, 16, 128), F32),
         "in_sem": dma((2,)),
         "w_sem": dma((2, len(WEIGHTS))),
         "w_send": dma((len(WEIGHTS),)),
-        "send": dma((UNITS, len(COPIES))),
-        "recv": dma((UNITS, len(COPIES))),
-        "gain_send": dma((6,)),
-        "gain_recv": dma((6,)),
+        "sent": dma((UNITS,)),
+        "recv": dma((UNITS, 7)),
+        "core_sent": dma((UNITS,)),
+        "core_recv": dma((UNITS,)),
+        "out_sent": dma((UNITS,)),
+        "out_recv": dma((UNITS,)),
+        "gain_send": dma((5,)),
+        "gain_recv": dma((5,)),
         "y_sem": dma((3,)),
         "dx_sem": dma((3,)),
     }
@@ -817,7 +689,7 @@
     count = mesh.shape["dp"]
 
     def per_device(tokens, sample_ids, cotangent, *weights):
-        units, rows_out, dx_out, gains = layers(2, tokens, sample_ids, cotangent, *weights)
+        units, rows_out, dx_out, gains = layers(3, tokens, sample_ids, cotangent, *weights)
         outs = spread(units, rows_out, dx_out, gains)
         if count > GROUP:
             members = [[g * GROUP + i for g in range(count // GROUP)] for i in range(GROUP)]

time: 127 us -> 104 us (0.82)
  Pallas kernels: 121 us -> 103 us
  local copies, waits for them, and re-layouts: 4.94 us -> 0 us
    pallas_call x1, Pallas kernels: 117 us -> 95.1 us  [layers(): pl.pallas_call(functools.partial(kernel, names, lag), out_shape=list(outp...]
    unnamed x8 -> x0, local copies, waits for them, and re-layouts: 4.94 us -> none
    pallas_call x1, Pallas kernels: 4.88 us -> 7.93 us  [spread(): pl.pallas_call(spread_kernel, grid=(6,), in_specs=[pl.BlockSpec((1, UNIT,...]
where the time goes in v2:
time: 104 us
  Pallas kernels  103 us (99%)
    pallas_call x1, Pallas kernels, layers(): pl.pallas_call(functools.partial(kernel, names, lag), out_shape=list(outp...  95.1 us
    pallas_call x1, Pallas kernels, spread(): pl.pallas_call(spread_kernel, grid=(6,), in_specs=[pl.BlockSpec((1, UNIT,...  7.93 us

profile of v2, /device:TPU:0, one launch (start us, length us, event | category | flops | bytes accessed | tf_op | source)
XLA Modules:
  0.0 103.7 jit_solution(6002905563473653570)
XLA Ops:
  0.6 95.1 %shard_map.203 = (bf16[6,2304,128]{2,1,0:T(8,128)(2,1)}, bf16[2,512,384]{2,1,0:T(8,128)(2,1)}, bf16[2,512,384]{2,1,0:T(8,128)(2,1)}, f32[8,128]{1,0:T(8,128)}) custom-call(bf16[2,512,384]{2,1,0:T(8,128)(2,1)} %refs_0_.1, bf16[2,512,384]{2,1,0:T(8,128)(2,1)} %refs_1_.1, f32[1,384]{1,0:T(1,128)} %refs_2_.1, bf16[1,384,384]{2,1,0:T(8,128)(2,1)} %refs_3_.1, ...), custom_call_target="tpu_custom_call" | custom-call | flops 15000000512 | bytes 10000000 | tf_op jit(solution)/shard_map/pallas_call | solution.py:675
  95.8 7.9 %shard_map.204 = (bf16[1,2,512,384]{3,2,1,0:T(8,128)(2,1)}, f32[1,2,512,384]{3,2,1,0:T(8,128)}, f32[1,384]{1,0:T(1,128)}, f32[1,384,384]{2,1,0:T(8,128)}, f32[1,...) custom-call(bf16[6,2304,128]{2,1,0:T(8,128)(2,1)} %get-tuple-element, ...), custom_call_target="tpu_custom_call" | custom-call | tf_op jit(solution)/shard_map/pallas_call | solution.py:584

commit v3 on v2

v3 whole, which is shorter than its diff:
```python
import functools
import types

import jax
import jax.numpy as jnp
from jax import lax
from jax.experimental import pallas as pl
from jax.experimental.pallas import tpu as pltpu
from jax.sharding import PartitionSpec as P

MESH = pl.DeviceIdType.MESH
BF = jnp.bfloat16
F32 = jnp.float32
HEADS = 6
HEAD_DIM = 64
NORM_EPS = 1e-05
MASKED = -1e30
GROUP = 16

SEQ = 512
DIM = 384
FF = 1024
HALF = SEQ // 2
CHUNK = FF // 4
UNITS = 12
UNIT = 2304
SHARE = UNIT // 2
PIECE = SHARE // 3
SLOTS = 15
WHEN = (
    (2, 6, 11, 17, 21, 25, 34, 52),
    (4, 8, 13, 17, 22, 28, 37, 58),
    (6, 12, 16, 20, 24, 29, 40, 50),
    (8, 12, 17, 21, 25, 35, 46, 61),
    (14, 18, 22, 26, 31, 37, 44, 63),
    (15, 19, 24, 28, 33, 40, 48, 69),
)
HALVES = (PIECE // 2, PIECE // 4, PIECE // 8)
STAGES = 8
FLAT = (PIECE // 2, PIECE // 4, PIECE // 4, PIECE // 4, PIECE // 4, PIECE // 4, PIECE // 2)
TALL = (PIECE // 2, PIECE // 4, PIECE // 8, PIECE // 8, PIECE // 8, PIECE // 4, PIECE // 2)
FLAT_LAND = sum(FLAT[:4])
LAND_ROWS = 2 * FLAT_LAND + sum(TALL[:4])


def mm(a, b):
    return lax.dot_general(a, b, (((1,), (0,)), ((), ())), preferred_element_type=F32)


def mm_nt(a, b):
    return lax.dot_general(a, b, (((1,), (1,)), ((), ())), preferred_element_type=F32)


def mm_tn(a, b):
    return lax.dot_general(a, b, (((0,), (0,)), ((), ())), preferred_element_type=F32)


def rsqrt_mean(values):
    return lax.rsqrt(jnp.mean(values * values, axis=-1, keepdims=True) + NORM_EPS)


PARTS = [(pair, block) for pair in range(HEADS // 2) for block in range(2)]


def lanes(pair, part=0):
    return pl.ds(part * DIM + pair * 2 * HEAD_DIM, 2 * HEAD_DIM)


def rows(start, size):
    return pl.ds(pl.multiple_of(start, 16), size)


class Links:
    def __init__(self, s):
        self.s = s
        self.c = lax.axis_index("section")
        self.dp = lax.axis_index("dp")
        local = lax.rem(self.dp, GROUP)
        x = lax.rem(local, 2)
        y = lax.rem(lax.div(local, 2), 2)
        z = lax.div(local, 4)
        p = lax.rem(z, 2)
        q = lax.div(z, 2)
        c = self.c
        self.middle = (z == 1) | (z == 2)
        self.end = (z == 0) | (z == 3)
        self.to_core = (1 - c, self.dp)
        step_x, step_y = 1 - 2 * x, 2 - 4 * y
        self.to_x = (c, self.dp + step_x)
        self.to_y = (c, self.dp + step_y)
        self.to_p = (c, self.dp + 4 - 8 * p)
        self.to_q = (c, self.dp + 8 - 16 * q)
        self.to_m = (c, self.dp + 4 - 8 * q)
        along_x, along_y, along_p = (x, self.to_x), (y, self.to_y), (p, self.to_p)
        one = (x + c * (y - x), (c, self.dp + step_x + c * (step_y - step_x)))
        two = (y + c * (x - y), (c, self.dp + step_y + c * (step_x - step_y)))
        orders = ((along_x, along_y), (along_y, along_x), (along_p, one, two))
        self.pieces = []
        for index, order in enumerate(orders):
            starts = [index * PIECE]
            for (bit, _), size in zip(order, HALVES):
                starts.append(starts[-1] + bit * size)
            self.pieces.append((index, order, starts))

    def meet(self):
        barrier = pltpu.get_barrier_semaphore()
        for target in (self.to_core, self.to_x, self.to_y, self.to_p, self.to_q):
            pl.semaphore_signal(barrier, inc=1, device_id=target, device_id_type=MESH)

        @pl.when(self.middle)
        def _():
            pl.semaphore_signal(barrier, inc=1, device_id=self.to_m, device_id_type=MESH)

    def met(self):
        barrier = pltpu.get_barrier_semaphore()

        @pl.when(self.middle)
        def _():
            pl.semaphore_wait(barrier, 6)

        @pl.when(self.end)
        def _():
            pl.semaphore_wait(barrier, 5)

    def landing(self, index, step):
        table = FLAT if index < 2 else TALL
        return pl.ds(index * FLAT_LAND + sum(table[:step]), table[step])

    def send(self, u, piece, step):
        index, order, starts = piece
        s = self.s
        table = FLAT if index < 2 else TALL
        halvings = len(order)
        if step < halvings:
            bit, target = order[step]
            src = s.part.at[u, rows(starts[step] + (1 - bit) * table[step], table[step])]
        elif step < 4:
            target = self.to_p if step == 2 else self.to_m if index < 2 else self.to_q
            src = s.part.at[u, rows(starts[halvings], table[step])]
        else:
            back = min(6 - step, halvings)
            target = order[back][1] if back < halvings else self.to_p
            src = s.done.at[u, rows(starts[min(back + 1, halvings)], table[step])]
        pltpu.make_async_remote_copy(
            src_ref=src,
            dst_ref=s.land.at[u, self.landing(index, step)] if step < 4 else src,
            send_sem=s.sent.at[u],
            recv_sem=s.recv.at[u, step],
            device_id=target,
            device_id_type=MESH,
        ).start()

    def wait(self, u, step, size, sent=False):
        some = self.s.own.at[u, pl.ds(0, size)]
        copy = pltpu.make_async_remote_copy(
            src_ref=some,
            dst_ref=some,
            send_sem=self.s.sent.at[u],
            recv_sem=self.s.recv.at[u, step],
            device_id=self.to_core,
            device_id_type=MESH,
        )
        copy.wait_send() if sent else copy.wait_recv()

    def add(self, u, piece, step):
        index, order, starts = piece
        s = self.s
        table = FLAT if index < 2 else TALL
        here = rows(starts[min(step + 1, len(order))], table[step])
        total = s.part[u, here] + s.land[u, self.landing(index, step)]
        if step < 3:
            s.part[u, here] = total
        else:
            s.done[u, here] = total

    def core_copy(self, u):
        return pltpu.make_async_remote_copy(
            src_ref=self.s.own.at[u, rows((1 - self.c) * SHARE, SHARE)],
            dst_ref=self.s.part.at[u],
            send_sem=self.s.core_sent.at[u],
            recv_sem=self.s.core_recv.at[u],
            device_id=self.to_core,
            device_id_type=MESH,
        )

    def result(self, k):
        return self.s.grads_out.at[k, rows(self.c * SHARE, SHARE)]

    def result_local(self, u, k):
        return pltpu.make_async_copy(self.s.done.at[u], self.result(k), self.s.out_sent.at[u])

    def result_copy(self, u, k):
        return pltpu.make_async_remote_copy(
            src_ref=self.s.done.at[u],
            dst_ref=self.result(k),
            send_sem=self.s.out_sent.at[u],
            recv_sem=self.s.out_recv.at[u],
            device_id=self.to_core,
            device_id_type=MESH,
        )

    def stage(self, step, u, k, layer):
        s = self.s
        flat, tall = self.pieces[:2], self.pieces[2]
        both, everything = 2 * FLAT[2] + TALL[2], self.pieces
        if step == 0:
            self.core_copy(u).wait_recv()
            s.part[u] = s.part[u] + s.own[u, rows(self.c * SHARE, SHARE)]
            for piece in everything:
                self.send(u, piece, 0)
        elif step == 1:
            self.wait(u, 0, 3 * FLAT[0])
            for piece in everything:
                self.add(u, piece, 0)
                self.send(u, piece, 1)
        elif step == 2:
            self.wait(u, 1, 3 * FLAT[1])
            for piece in everything:
                self.add(u, piece, 1)
            self.send(u, tall, 2)

            @pl.when(self.end)
            def _():
                for piece in flat:
                    self.send(u, piece, 2)
        elif step == 3:
            pl.when(self.middle)(lambda: self.wait(u, 2, both))
            pl.when(self.end)(lambda: self.wait(u, 2, TALL[2]))
            self.add(u, tall, 2)
            self.send(u, tall, 3)

            @pl.when(self.middle)
            def _():
                for piece in flat:
                    self.add(u, piece, 2)
                    self.send(u, piece, 3)
        elif step == 4:
            pl.when(self.middle)(lambda: self.wait(u, 3, both))
            pl.when(self.end)(lambda: self.wait(u, 3, TALL[3]))
            self.add(u, tall, 3)
            self.send(u, tall, 4)

            @pl.when(self.middle)
            def _():
                for piece in flat:
                    self.add(u, piece, 3)
                    self.send(u, piece, 4)
                    self.send(u, piece, 5)
        elif step == 5:
            pl.when(self.middle)(lambda: self.wait(u, 4, TALL[4]))
            pl.when(self.end)(lambda: self.wait(u, 4, both))
            self.send(u, tall, 5)

            @pl.when(self.end)
            def _():
                for piece in flat:
                    self.send(u, piece, 5)
        elif step == 6:
            self.wait(u, 5, 3 * FLAT[5])
            for piece in everything:
                self.send(u, piece, 6)
        elif step == 7:
            self.wait(u, 6, 3 * FLAT[6])
            pl.when(layer == self.c)(lambda: self.result_local(u, k).start())
            pl.when(layer != self.c)(lambda: self.result_copy(u, k).start())
            self.core_copy(u).wait_send()
            sent = sum(TALL) + 2 * (FLAT[0] + FLAT[1] + FLAT[5] + FLAT[6])
            pl.when(self.middle)(lambda: self.wait(u, 0, sent + 2 * (FLAT[3] + FLAT[4]), sent=True))
            pl.when(self.end)(lambda: self.wait(u, 0, sent + 2 * FLAT[2], sent=True))

    def settle(self, u):
        layer, k = 1 - lax.div(u, 6), lax.rem(u, 6)

        @pl.when(layer == self.c)
        def _():
            self.result_local(u, k).wait()
            self.result_copy(u, k).wait_recv()

        @pl.when(layer != self.c)
        def _():
            self.result_copy(u, k).wait_send()

    def sum_gains(self, step):
        s = self.s
        total = s.gain_sum
        targets = (self.to_core, self.to_x, self.to_y, self.to_p, self.to_q)

        def copy(index):
            return pltpu.make_async_remote_copy(
                src_ref=total.at[index],
                dst_ref=s.gain_land.at[index],
                send_sem=s.gain_send.at[index],
                recv_sem=s.gain_recv.at[index],
                device_id=targets[index],
                device_id_type=MESH,
            )

        if step > 0:
            copy(step - 1).wait()
            total[step] = total[step - 1] + s.gain_land[step - 1]
        if step < 5:
            copy(step).start()


WEIGHTS = ("first_gain", "query", "key", "value", "output", "second_gain", "gate", "up", "down")


def kernel(names, *refs):
    s = types.SimpleNamespace(**dict(zip(names, refs)))
    links = Links(s)
    c = links.c
    links.meet()

    token_copy = pltpu.make_async_copy(s.tokens.at[c], s.tok, s.in_sem.at[0])
    token_copy.start()
    cot_copy = pltpu.make_async_copy(s.cotangent.at[c], s.cot, s.in_sem.at[1])
    cot_copy.start()

    def place(name, layer):
        where = {
            "first_gain": lambda: s.gain1.at[layer],
            "query": lambda: s.wqkv.at[layer, :, pl.ds(0, DIM)],
            "key": lambda: s.wqkv.at[layer, :, pl.ds(DIM, DIM)],
            "value": lambda: s.wqkv.at[layer, :, pl.ds(2 * DIM, DIM)],
            "output": lambda: s.wo.at[layer],
            "second_gain": lambda: s.gain2.at[layer],
            "gate": lambda: s.wg.at[layer],
            "up": lambda: s.wu.at[layer],
            "down": lambda: s.wd.at[layer],
        }
        return where[name]()

    def source(name):
        ref = getattr(s, "in_" + name)
        return ref if name.endswith("gain") else ref.at[0]

    def weight_local(name, layer):
        index = WEIGHTS.index(name)
        return pltpu.make_async_copy(source(name), place(name, layer), s.w_sem.at[layer, index])

    def weight_copy(name, layer):
        index = WEIGHTS.index(name)
        return pltpu.make_async_remote_copy(
            src_ref=source(name),
            dst_ref=place(name, layer),
            send_sem=s.w_send.at[index],
            recv_sem=s.w_sem.at[layer, index],
            device_id=links.to_core,
            device_id_type=MESH,
        )

    def need(layer, *which):
        for name in which:
            weight_local(name, layer).wait()

    for name in WEIGHTS:
        weight_local(name, c).start()

    ids = s.sample_ids[pl.ds(c, 1), :].astype(F32)
    count = [jnp.sum(jnp.where(ids == v, 1.0, 0.0), axis=-1, keepdims=True) for v in range(3)]
    first = jnp.where(
        count[0] == HALF,
        0.0,
        jnp.where(
            count[1] == HALF,
            count[0],
            jnp.where(count[2] == HALF, count[0] + count[1], count[0] + count[1] + count[2]),
        ),
    ).astype(jnp.int32)
    down_iota = lax.broadcasted_iota(jnp.int32, (SEQ, SEQ), 0)
    lane_iota = lax.broadcasted_iota(jnp.int32, (SEQ, SEQ), 1)
    moved = down_iota + first
    moved = jnp.where(moved >= SEQ, moved - SEQ, moved)
    perm = jnp.where(lane_iota == moved, 1.0, 0.0)
    ids_down = jnp.sum(perm[HALF:] * ids, axis=-1, keepdims=True)
    s.perm[...] = perm.astype(BF)
    moved = lane_iota + first
    moved = jnp.where(moved >= SEQ, moved - SEQ, moved)
    s.back[...] = jnp.where(down_iota == moved, 1.0, 0.0).astype(BF)
    ids_lane = mm(jnp.broadcast_to(ids, (16, SEQ)).astype(BF), s.back[:, HALF:])[:1]
    s.mask[...] = jnp.where(ids_down == ids_lane, 0.0, MASKED)

    token_copy.wait()
    s.x[0] = mm(s.perm[...], s.tok[...]).astype(BF)
    cot_copy.wait()
    s.dy[...] = mm(s.perm[...], s.cot[...]).astype(BF)

    links.met()
    for name in WEIGHTS[:6]:
        weight_copy(name, c).start()

    head0 = lax.broadcasted_iota(jnp.int32, (HALF, 128), 1) < HEAD_DIM

    def of_head(values, h):
        return jnp.where(head0 if h == 0 else ~head0, values, jnp.zeros_like(values))

    def output_row(layer, src, out, sems):
        @pl.when(layer == c)
        def _():
            pltpu.make_async_copy(src, out.at[c], sems.at[0]).start()

        @pl.when(layer != c)
        def _():
            pltpu.make_async_remote_copy(
                src_ref=src, dst_ref=out.at[c], send_sem=sems.at[1], recv_sem=sems.at[2],
                device_id=links.to_core, device_id_type=MESH,
            ).start()

    def output_settle(src, out, sems):
        pltpu.make_async_copy(src, out.at[c], sems.at[0]).wait()
        pltpu.make_async_remote_copy(
            src_ref=src, dst_ref=out.at[c], send_sem=sems.at[1], recv_sem=sems.at[2],
            device_id=links.to_core, device_id_type=MESH,
        ).wait()

    def forward(layer):
        need(layer, "first_gain", "query", "key", "value")
        x = s.x[layer].astype(F32)
        r = rsqrt_mean(x)
        s.r1[layer] = r
        a = (x * r * s.gain1[layer]).astype(BF)
        s.a[layer] = a
        for lo, hi in ((0, 512), (512, 1024), (1024, 1152)):
            part = mm(a, s.wqkv[layer, :, lo:hi])
            if lo == 0:
                s.qkv[layer, :, :DIM] = (part[:, :DIM] * HEAD_DIM ** (-0.5)).astype(BF)
                s.qkv[layer, :, DIM:hi] = part[:, DIM:].astype(BF)
            else:
                s.qkv[layer, :, lo:hi] = part.astype(BF)

        @pl.when(layer == 0)
        def _():
            for name in WEIGHTS[6:]:
                weight_copy(name, c).start()


        for pair, block in PARTS:
            at = pl.ds(block * HALF, HALF)
            q, k, v = [s.qkv[layer, at, lanes(pair, part)] for part in range(3)]
            outs = []
            for h in range(2):
                score = mm_nt(q, of_head(k, h))
                if block == 1:
                    score = score + s.mask[...]
                expo = jnp.exp(score - jnp.max(score, axis=-1, keepdims=True)).astype(BF)
                s.e[layer, pair * 4 + block * 2 + h] = expo
                outs.append(mm(expo, jnp.where(head0 if h == 0 else ~head0, v, jnp.ones_like(v))))
            inverse = 1.0 / pltpu.roll(jnp.where(head0, outs[1], outs[0]), HEAD_DIM, 1)
            s.inverse[layer, pair * 2 + block] = inverse
            s.o[layer, at, lanes(pair)] = (jnp.where(head0, outs[0], outs[1]) * inverse).astype(BF)

        need(layer, "output", "second_gain")
        x1 = x + mm(s.o[layer], s.wo[layer])
        s.x1[layer] = x1
        r = rsqrt_mean(x1)
        s.r2[layer] = r
        s.b[layer] = (x1 * r * s.gain2[layer]).astype(BF)
        need(layer, "gate", "up", "down")

    def hidden(layer, j):
        at = pl.ds(j * CHUNK if isinstance(j, int) else pl.multiple_of(j * CHUNK, CHUNK), CHUNK)
        b = s.b[layer]
        g = mm(b, s.wg[layer, :, at])
        u = mm(b, s.wu[layer, :, at])
        sig = 1.0 / (1.0 + jnp.exp(-g))
        return at, g, u, sig

    def unroll(layer, low, out, dst, sems):
        out[layer] = mm(s.back[...], low[...]).astype(BF)
        output_row(layer, out.at[layer], dst, sems)

    @pl.loop(0, 2)
    def _(layer):
        forward(layer)

        @pl.when(layer == 0)
        def _():
            s.acc[...] = s.x1[0]

            @pl.loop(0, 4)
            def _(j):
                at, g, u, sig = hidden(0, j)
                f = (g * sig * u).astype(BF)
                s.acc[...] += mm(f, s.wd[0, at, :])

            s.x[1] = s.acc[...].astype(BF)

    def put(u, start, values):
        size, width = values.shape
        for lo in range(0, width, 128):
            s.own[u, pl.ds(start, size), :] = values[:, lo : lo + 128].astype(BF)
            start += size
        return start

    def put_gain(layer, which, values):
        for i in range(DIM // 128):
            s.gain_sum[0, pl.ds(layer * 8 + which * 4 + i, 1), :] = values[:, i * 128 : (i + 1) * 128]

    def slot(turn, index):
        found = []
        for k in range(6):
            for step in range(STAGES):
                before, place = divmod(WHEN[k][step], SLOTS)
                if place == index and before < 2:
                    found.append((-step, -before, k))
        for step, before, k in sorted(found):
            if before == 0:
                links.stage(-step, 6 * turn + k, k, 1 - turn)
            else:
                pl.when(turn == 1)(functools.partial(links.stage, -step, k, k, 1))

    def after_compute():
        found = []
        for turn in range(2):
            for k in range(6):
                for step in range(STAGES):
                    place = turn * SLOTS + WHEN[k][step]
                    if place >= 2 * SLOTS:
                        found.append((place, -step, 6 * turn + k))
        return [(-step, u) for _, step, u in sorted(found)]

    def made(u):
        links.core_copy(u).start()

    s.gain_sum[0] = jnp.zeros((16, 128), F32)

    @pl.loop(0, 2)
    def _(turn):
        layer = 1 - turn
        base = turn * 6
        s.bt[...] = s.b[layer].T
        s.db[...] = jnp.zeros((SEQ, DIM), F32)

        for j in range(4):
            at, g, u, sig = hidden(layer, j)
            silu = g * sig
            f = (silu * u).astype(BF)
            dy = s.dy[...]
            df = mm_nt(dy, s.wd[layer, at, :])
            dg = (df * u * sig * (1.0 + g * (1.0 - sig))).astype(BF)
            du = (df * silu).astype(BF)
            s.f[:, at] = f
            nxt = put(base + j, 0, mm_tn(f, dy))
            nxt = put(base + j, nxt, mm(s.bt[...], dg))
            put(base + j, nxt, mm(s.bt[...], du))
            made(base + j)
            slot(turn, 2 * j)
            s.db[...] += mm_nt(dg, s.wg[layer, :, at]) + mm_nt(du, s.wu[layer, :, at])
            slot(turn, 2 * j + 1)

        @pl.when(layer == 1)
        def _():
            s.y[...] = (s.x1[1] + mm(s.f[...], s.wd[1])).astype(BF)

        db = s.db[...]
        r = s.r2[layer]
        normed = s.x1[layer] * r
        put_gain(layer, 1, jnp.sum(db * normed, axis=0, keepdims=True))
        part = db * s.gain2[layer]
        dx1 = s.dy[...].astype(F32) + r * (part - normed * jnp.mean(part * normed, axis=-1, keepdims=True))
        s.dx1[...] = dx1
        low = dx1.astype(BF)
        nxt = put(base + 4, 0, mm_tn(s.o[layer], low))
        s.do[...] = mm_nt(low, s.wo[layer]).astype(BF)
        slot(turn, 8)

        for pair, block in PARTS:
            at = pl.ds(block * HALF, HALF)
            q, k, v = [s.qkv[layer, at, lanes(pair, part)] for part in range(3)]
            do = s.do[at, lanes(pair)].astype(F32) * s.inverse[layer, pair * 2 + block]
            inner = do * s.o[layer, at, lanes(pair)].astype(F32)
            do = do.astype(BF)
            q_t, do_t = q.T, do.T
            dq, dk_t, dv_t = None, [], []
            for h in range(2):
                mine = slice(h * HEAD_DIM, (h + 1) * HEAD_DIM)
                expo = s.e[layer, pair * 4 + block * 2 + h]
                dv_t.append(mm(do_t[mine], expo))
                dp = mm_nt(do, of_head(v, h))
                ds = expo.astype(F32) * (dp - jnp.sum(of_head(inner, h), axis=-1, keepdims=True))
                ds = ds.astype(BF)
                term = mm(ds, of_head(k, h))
                dk_t.append(mm(q_t[mine], ds))
                dq = term if h == 0 else dq + term
            s.dqkv[at, lanes(pair, 0)] = (dq * HEAD_DIM ** (-0.5)).astype(BF)
            s.dqkv[at, lanes(pair, 1)] = jnp.concatenate(dk_t, 0).astype(BF).T
            s.dqkv[at, lanes(pair, 2)] = jnp.concatenate(dv_t, 0).astype(BF).T
            if block == 1:
                slot(turn, 9 + pair)

        s.at[...] = s.a[layer].T
        put(base + 4, nxt, mm(s.at[...], s.dqkv[:, :DIM]))
        made(base + 4)
        slot(turn, 12)
        nxt = put(base + 5, 0, mm(s.at[...], s.dqkv[:, DIM : 2 * DIM]))
        put(base + 5, nxt, mm(s.at[...], s.dqkv[:, 2 * DIM :]))
        made(base + 5)
        slot(turn, 13)

        da = mm_nt(s.dqkv[...], s.wqkv[layer])
        r = s.r1[layer]
        normed = s.x[layer].astype(F32) * r
        put_gain(layer, 0, jnp.sum(da * normed, axis=0, keepdims=True))
        part = da * s.gain1[layer]
        dx = s.dx1[...] + r * (part - normed * jnp.mean(part * normed, axis=-1, keepdims=True))
        low = dx.astype(BF)
        s.dy[...] = low
        s.dx[layer] = low
        slot(turn, 14)

    left = after_compute()
    beside = {2 + 2 * i: functools.partial(unroll, *row) for i, row in enumerate((
        (0, s.dx.at[0], s.dx_row, s.dx_out, s.dx_sem),
        (1, s.dx.at[1], s.dx_row, s.dx_out, s.dx_sem),
        (0, s.x.at[1], s.y_row, s.rows_out, s.y_sem),
        (1, s.y, s.y_row, s.rows_out, s.y_sem),
    ))}
    gap = max((len(left) - 4) // 5, 1)
    for index, (step, u) in enumerate(left):
        if index % gap == 0 and index // gap < 6:
            links.sum_gains(index // gap)
        links.stage(step, u, u % 6, 1 - u // 6)
        if index in beside:
            beside[index]()

    s.gains_out[...] = s.gain_sum[5, pl.ds(pl.multiple_of(c * 8, 8), 8), :]

    @pl.loop(0, UNITS)
    def _(u):
        links.settle(u)

    for index, name in enumerate(WEIGHTS):
        weight_copy(name, c).wait_send()
    output_settle(s.y_row.at[0], s.rows_out, s.y_sem)
    output_settle(s.dx_row.at[0], s.dx_out, s.dx_sem)


def spread_kernel(*refs):
    s = types.SimpleNamespace(**dict(zip(SPREAD_NAMES, refs)))

    def load(index, src, dst):
        return pltpu.make_async_copy(src, dst, s.in_sem.at[index])

    def store(index, src, dst):
        return pltpu.make_async_copy(src, dst, s.out_sem.at[index])

    unit_loads = [load(u, s.units.at[u], s.unit.at[u]) for u in range(6)]
    dx_load = load(6, s.dx_in, s.dx)
    rows_load = load(7, s.rows_in, s.rows)
    stores = []
    for u in (4, 5, 0, 1, 2, 3):
        unit_loads[u].start()
    rows_load.start()
    dx_load.start()

    def panels(u, first, size, wide, dst):
        for p in range(wide):
            dst[:, p * 128 : (p + 1) * 128] = s.unit[u, pl.ds((first + p) * size, size), :].astype(F32)

    squares = ((4, 0, s.output), (4, 3, s.query), (5, 0, s.key), (5, 3, s.value))
    for index, (u, first, out) in enumerate(squares):
        if first == 0:
            unit_loads[u].wait()
        panels(u, first, DIM, 3, s.square.at[index])
        stores.append(store(1 + index, s.square.at[index], out.at[0]))
        stores[-1].start()
    for p in range(3):
        s.vectors[0:1, p * 128 : (p + 1) * 128] = s.gains_in[p : p + 1, :]
        s.vectors[8:9, p * 128 : (p + 1) * 128] = s.gains_in[4 + p : 5 + p, :]
    stores.append(store(5, s.vectors.at[pl.ds(0, 1)], s.first))
    stores.append(store(6, s.vectors.at[pl.ds(8, 1)], s.second))
    stores[-2].start()
    stores[-1].start()
    rows_load.wait()
    stores.append(store(0, s.rows, s.rows_out.at[0]))
    stores[-1].start()
    dx_load.wait()

    @pl.loop(0, 2)
    def _(row):
        s.dx_wide[row] = s.dx[row].astype(F32)

    stores.append(store(7, s.dx_wide, s.dx_out.at[0]))
    stores[-1].start()

    def chunk_stores(u):
        at = pl.ds(pl.multiple_of(u * CHUNK, CHUNK), CHUNK)
        return (
            store(8 + u, s.down_wide.at[u], s.down.at[0, at, :]),
            store(12 + u, s.gate_wide.at[u], s.gate.at[0, :, at]),
            store(16 + u, s.up_wide.at[u], s.up.at[0, :, at]),
        )

    @pl.loop(0, 4)
    def _(u):
        load(u, s.units.at[u], s.unit.at[u]).wait()
        panels(u, 0, CHUNK, 3, s.down_wide.at[u])
        panels(u, 2, DIM, 2, s.gate_wide.at[u])
        panels(u, 4, DIM, 2, s.up_wide.at[u])
        for one in chunk_stores(u):
            one.start()

    for one in stores:
        one.wait()

    @pl.loop(0, 4)
    def _(u):
        for one in chunk_stores(u):
            one.wait()


SPREAD_OUTS = {
    "rows_out": ((1, 2, SEQ, DIM), BF),
    "dx_out": ((1, 2, SEQ, DIM), F32),
    "first": ((1, DIM), F32),
    "query": ((1, DIM, DIM), F32),
    "key": ((1, DIM, DIM), F32),
    "value": ((1, DIM, DIM), F32),
    "output": ((1, DIM, DIM), F32),
    "second": ((1, DIM), F32),
    "gate": ((1, DIM, FF), F32),
    "up": ((1, DIM, FF), F32),
    "down": ((1, FF, DIM), F32),
}
SPREAD_SCRATCH = {
    "unit": pltpu.VMEM((6, UNIT, 128), BF),
    "rows": pltpu.VMEM((2, SEQ, DIM), BF),
    "dx": pltpu.VMEM((2, SEQ, DIM), BF),
    "dx_wide": pltpu.VMEM((2, SEQ, DIM), F32),
    "square": pltpu.VMEM((4, DIM, DIM), F32),
    "vectors": pltpu.VMEM((16, DIM), F32),
    "down_wide": pltpu.VMEM((4, CHUNK, DIM), F32),
    "gate_wide": pltpu.VMEM((4, DIM, CHUNK), F32),
    "up_wide": pltpu.VMEM((4, DIM, CHUNK), F32),
    "in_sem": pltpu.SemaphoreType.DMA((8,)),
    "out_sem": pltpu.SemaphoreType.DMA((20,)),
}
SPREAD_NAMES = ["units", "rows_in", "dx_in", "gains_in", *SPREAD_OUTS, *SPREAD_SCRATCH]


def spread(units, rows_in, dx_in, gains):
    anywhere = pl.BlockSpec(memory_space=pl.ANY)
    return pl.pallas_call(
        spread_kernel,
        in_specs=[anywhere] * 3 + [pl.BlockSpec(memory_space=pltpu.VMEM)],
        out_specs=[anywhere] * len(SPREAD_OUTS),
        out_shape=[jax.ShapeDtypeStruct(*shape) for shape in SPREAD_OUTS.values()],
        scratch_shapes=list(SPREAD_SCRATCH.values()),
        compiler_params=pltpu.CompilerParams(vmem_limit_bytes=62 * 2**20),
    )(units, rows_in, dx_in, gains)


def layers(tokens, sample_ids, cotangent, *weights):
    anywhere = pl.BlockSpec(memory_space=pl.ANY)
    vmem = pl.BlockSpec(memory_space=pltpu.VMEM)
    inputs = ["tokens", "cotangent"] + ["in_" + name for name in WEIGHTS] + ["sample_ids"]
    outputs = {
        "grads_out": jax.ShapeDtypeStruct((UNITS // 2, UNIT, 128), BF),
        "rows_out": jax.ShapeDtypeStruct((2, SEQ, DIM), BF),
        "dx_out": jax.ShapeDtypeStruct((2, SEQ, DIM), BF),
        "gains_out": jax.ShapeDtypeStruct((8, 128), F32),
    }
    dma = pltpu.SemaphoreType.DMA
    scratch = {
        "tok": pltpu.VMEM((SEQ, DIM), BF),
        "cot": pltpu.VMEM((SEQ, DIM), BF),
        "gain1": pltpu.VMEM((2, 1, DIM), F32),
        "gain2": pltpu.VMEM((2, 1, DIM), F32),
        "wqkv": pltpu.VMEM((2, DIM, 3 * DIM), BF),
        "wo": pltpu.VMEM((2, DIM, DIM), BF),
        "wg": pltpu.VMEM((2, DIM, FF), BF),
        "wu": pltpu.VMEM((2, DIM, FF), BF),
        "wd": pltpu.VMEM((2, FF, DIM), BF),
        "perm": pltpu.VMEM((SEQ, SEQ), BF),
        "back": pltpu.VMEM((SEQ, SEQ), BF),
        "mask": pltpu.VMEM((HALF, HALF), F32),
        "x": pltpu.VMEM((2, SEQ, DIM), BF),
        "a": pltpu.VMEM((2, SEQ, DIM), BF),
        "qkv": pltpu.VMEM((2, SEQ, 3 * DIM), BF),
        "e": pltpu.VMEM((2, 2 * HEADS, HALF, HALF), BF),
        "inverse": pltpu.VMEM((2, HEADS, HALF, 128), F32),
        "f": pltpu.VMEM((SEQ, FF), BF),
        "o": pltpu.VMEM((2, SEQ, DIM), BF),
        "x1": pltpu.VMEM((2, SEQ, DIM), F32),
        "b": pltpu.VMEM((2, SEQ, DIM), BF),
        "r1": pltpu.VMEM((2, SEQ, 1), F32),
        "r2": pltpu.VMEM((2, SEQ, 1), F32),
        "acc": pltpu.VMEM((SEQ, DIM), F32),
        "bt": pltpu.VMEM((DIM, SEQ), BF),
        "at": pltpu.VMEM((DIM, SEQ), BF),
        "db": pltpu.VMEM((SEQ, DIM), F32),
        "dy": pltpu.VMEM((SEQ, DIM), BF),
        "dx1": pltpu.VMEM((SEQ, DIM), F32),
        "dx": pltpu.VMEM((2, SEQ, DIM), BF),
        "y": pltpu.VMEM((SEQ, DIM), BF),
        "do": pltpu.VMEM((SEQ, DIM), BF),
        "dqkv": pltpu.VMEM((SEQ, 3 * DIM), BF),
        "y_row": pltpu.VMEM((2, SEQ, DIM), BF),
        "dx_row": pltpu.VMEM((2, SEQ, DIM), BF),
        "own": pltpu.VMEM((UNITS, UNIT, 128), BF),
        "part": pltpu.VMEM((UNITS, SHARE, 128), BF),
        "land": pltpu.VMEM((UNITS, LAND_ROWS, 128), BF),
        "done": pltpu.VMEM((UNITS, SHARE, 128), BF),
        "gain_sum": pltpu.VMEM((6, 16, 128), F32),
        "gain_land": pltpu.VMEM((5, 16, 128), F32),
        "in_sem": dma((2,)),
        "w_sem": dma((2, len(WEIGHTS))),
        "w_send": dma((len(WEIGHTS),)),
        "sent": dma((UNITS,)),
        "recv": dma((UNITS, 7)),
        "core_sent": dma((UNITS,)),
        "core_recv": dma((UNITS,)),
        "out_sent": dma((UNITS,)),
        "out_recv": dma((UNITS,)),
        "gain_send": dma((5,)),
        "gain_recv": dma((5,)),
        "y_sem": dma((3,)),
        "dx_sem": dma((3,)),
    }
    names = inputs + list(outputs) + list(scratch)
    return pl.pallas_call(
        functools.partial(kernel, names),
        out_shape=list(outputs.values()),
        in_specs=[anywhere] * (len(inputs) - 1) + [vmem],
        out_specs=[anywhere, anywhere, anywhere, vmem],
        scratch_shapes=list(scratch.values()),
        compiler_params=pltpu.CompilerParams(
            collective_id=0, has_side_effects=True, vmem_limit_bytes=62 * 2**20
        ),
        cost_estimate=pl.CostEstimate(flops=15 * 10**9, bytes_accessed=10**7, transcendentals=4 * 10**6),
    )(tokens, cotangent, *weights, sample_ids)


def solution(mesh):
    count = mesh.shape["dp"]

    def per_device(tokens, sample_ids, cotangent, *weights):
        units, rows_out, dx_out, gains = layers(tokens, sample_ids, cotangent, *weights)
        outs = spread(units, rows_out, dx_out, gains)
        if count > GROUP:
            members = [[g * GROUP + i for g in range(count // GROUP)] for i in range(GROUP)]
            outs = list(outs[:2]) + list(lax.psum(tuple(outs[2:]), "dp", axis_index_groups=members))
        return tuple(outs)

    matrix = P("section", None, None)
    vector = P("section", None)
    rows4 = P("section", "dp", None, None)
    grads = (vector, matrix, matrix, matrix, matrix, vector, matrix, matrix, matrix)
    return jax.shard_map(
        per_device,
        mesh=mesh,
        in_specs=(P("dp", None, None), P("dp", None), P("dp", None, None)) + grads,
        out_specs=(rows4, rows4) + grads,
        check_vma=False,
    )
```

time: 104 us -> 89 us (0.86)
  Pallas kernels: 103 us -> 87.9 us
    pallas_call x2, Pallas kernels: 103 us -> 87.9 us  [the longest x1 81 us: layers(): pl.pallas_call(functools.partial(kernel, names), out_shape=list(outputs.v...]
where the time goes in v3:
time: 89 us; the launch traced here: 88.8 us
  Pallas kernels  87.9 us (99%)
    pallas_call x1, Pallas kernels, layers(): pl.pallas_call(functools.partial(kernel, names), out_shape=list(outputs.v...  81 us
    pallas_call x1, Pallas kernels, spread(): pl.pallas_call(spread_kernel, in_specs=[anywhere] * 3 + [pl.BlockSpec(mem...  6.94 us

profile of v3, /device:TPU:0, one launch (start us, length us, event | category | flops | bytes accessed | tf_op | source)
XLA Modules:
  0.0 88.8 jit_solution(9760729318628991447)
XLA Ops:
  0.6 81.0 %shard_map.203 = (bf16[6,2304,128]{2,1,0:T(8,128)(2,1)}, bf16[2,512,384]{2,1,0:T(8,128)(2,1)}, bf16[2,512,384]{2,1,0:T(8,128)(2,1)}, f32[8,128]{1,0:T(8,128)}) custom-call(bf16[2,512,384]{2,1,0:T(8,128)(2,1)} %refs_0_.1, bf16[2,512,384]{2,1,0:T(8,128)(2,1)} %refs_1_.1, f32[1,384]{1,0:T(1,128)} %refs_2_.1, bf16[1,384,384]{2,1,0:T(8,128)(2,1)} %refs_3_.1, ...), custom_call_target="tpu_custom_call" | custom-call | flops 15000000512 | bytes 10000000 | tf_op jit(solution)/shard_map/pallas_call | solution.py:821
  81.6 6.9 %shard_map.204 = (bf16[1,2,512,384]{3,2,1,0:T(8,128)(2,1)}, f32[1,2,512,384]{3,2,1,0:T(8,128)}, f32[1,384]{1,0:T(1,128)}, f32[1,384,384]{2,1,0:T(8,128)}, f32[1,...) custom-call(bf16[6,2304,128]{2,1,0:T(8,128)(2,1)} %get-tuple-element, ...), custom_call_target="tpu_custom_call" | custom-call | tf_op jit(solution)/shard_map/pallas_call | solution.py:743

commit v4 on v3

--- a/solution.py
+++ b/solution.py
@@ -177,7 +177,7 @@
         return pltpu.make_async_remote_copy(
             src_ref=self.s.own.at[u, rows((1 - self.c) * SHARE, SHARE)],
             dst_ref=self.s.part.at[u],
-            send_sem=self.s.core_sent.at[u],
+            send_sem=self.s.core_sent,
             recv_sem=self.s.core_recv.at[u],
             device_id=self.to_core,
             device_id_type=MESH,
@@ -187,14 +187,14 @@
         return self.s.grads_out.at[k, rows(self.c * SHARE, SHARE)]
 
     def result_local(self, u, k):
-        return pltpu.make_async_copy(self.s.done.at[u], self.result(k), self.s.out_sent.at[u])
+        return pltpu.make_async_copy(self.s.done.at[u], self.result(k), self.s.out_sent)
 
     def result_copy(self, u, k):
         return pltpu.make_async_remote_copy(
             src_ref=self.s.done.at[u],
             dst_ref=self.result(k),
-            send_sem=self.s.out_sent.at[u],
-            recv_sem=self.s.out_recv.at[u],
+            send_sem=self.s.out_sent,
+            recv_sem=self.s.out_recv,
             device_id=self.to_core,
             device_id_type=MESH,
         )
@@ -263,22 +263,21 @@
             self.wait(u, 6, 3 * FLAT[6])
             pl.when(layer == self.c)(lambda: self.result_local(u, k).start())
             pl.when(layer != self.c)(lambda: self.result_copy(u, k).start())
-            self.core_copy(u).wait_send()
             sent = sum(TALL) + 2 * (FLAT[0] + FLAT[1] + FLAT[5] + FLAT[6])
             pl.when(self.middle)(lambda: self.wait(u, 0, sent + 2 * (FLAT[3] + FLAT[4]), sent=True))
             pl.when(self.end)(lambda: self.wait(u, 0, sent + 2 * FLAT[2], sent=True))
 
-    def settle(self, u):
-        layer, k = 1 - lax.div(u, 6), lax.rem(u, 6)
-
-        @pl.when(layer == self.c)
-        def _():
-            self.result_local(u, k).wait()
-            self.result_copy(u, k).wait_recv()
-
-        @pl.when(layer != self.c)
-        def _():
-            self.result_copy(u, k).wait_send()
+    def settle(self):
+        def whole(refs, send_sem, recv_sem):
+            return pltpu.make_async_remote_copy(
+                src_ref=refs, dst_ref=refs, send_sem=send_sem, recv_sem=recv_sem,
+                device_id=self.to_core, device_id_type=MESH,
+            )
+
+        s = self.s
+        whole(s.part, s.core_sent, s.out_recv).wait_send()
+        whole(s.done, s.out_sent, s.out_recv).wait_send()
+        whole(s.done.at[pl.ds(0, UNITS // 2)], s.out_sent, s.out_recv).wait_recv()
 
     def sum_gains(self, step):
         s = self.s
@@ -303,6 +302,9 @@
 
 
 WEIGHTS = ("first_gain", "query", "key", "value", "output", "second_gain", "gate", "up", "down")
+EARLY = (("first_gain", 0), ("query", 0), ("key", 0), ("value", 0))
+LATE = (("output", 0), ("second_gain", 0)) + tuple((name, half) for half in range(2) for name in ("gate", "up", "down"))
+HANDED = EARLY + LATE
 
 
 def kernel(names, *refs):
@@ -316,7 +318,8 @@
     cot_copy = pltpu.make_async_copy(s.cotangent.at[c], s.cot, s.in_sem.at[1])
     cot_copy.start()
 
-    def place(name, layer):
+    def place(name, half, layer):
+        part = pl.ds(half * (FF // 2), FF // 2)
         where = {
             "first_gain": lambda: s.gain1.at[layer],
             "query": lambda: s.wqkv.at[layer, :, pl.ds(0, DIM)],
@@ -324,37 +327,40 @@
             "value": lambda: s.wqkv.at[layer, :, pl.ds(2 * DIM, DIM)],
             "output": lambda: s.wo.at[layer],
             "second_gain": lambda: s.gain2.at[layer],
-            "gate": lambda: s.wg.at[layer],
-            "up": lambda: s.wu.at[layer],
-            "down": lambda: s.wd.at[layer],
+            "gate": lambda: s.wg.at[layer, :, part],
+            "up": lambda: s.wu.at[layer, :, part],
+            "down": lambda: s.wd.at[layer, part, :],
         }
         return where[name]()
 
-    def source(name):
+    def source(name, half):
         ref = getattr(s, "in_" + name)
-        return ref if name.endswith("gain") else ref.at[0]
-
-    def weight_local(name, layer):
-        index = WEIGHTS.index(name)
-        return pltpu.make_async_copy(source(name), place(name, layer), s.w_sem.at[layer, index])
-
-    def weight_copy(name, layer):
-        index = WEIGHTS.index(name)
+        part = pl.ds(half * (FF // 2), FF // 2)
+        if name.endswith("gain"):
+            return ref
+        return ref.at[0, :, part] if name in ("gate", "up") else ref.at[0, part, :] if name == "down" else ref.at[0]
+
+    def weight_local(piece, layer):
+        sem = s.w_sem.at[layer, HANDED.index(piece)]
+        return pltpu.make_async_copy(source(*piece), place(*piece, layer), sem)
+
+    def weight_copy(piece, layer):
+        index = HANDED.index(piece)
         return pltpu.make_async_remote_copy(
-            src_ref=source(name),
-            dst_ref=place(name, layer),
+            src_ref=place(*piece, layer) if piece in EARLY else source(*piece),
+            dst_ref=place(*piece, layer),
             send_sem=s.w_send.at[index],
             recv_sem=s.w_sem.at[layer, index],
             device_id=links.to_core,
             device_id_type=MESH,
         )
 
-    def need(layer, *which):
-        for name in which:
-            weight_local(name, layer).wait()
-
-    for name in WEIGHTS:
-        weight_local(name, c).start()
+    def need(layer, *pieces):
+        for piece in pieces:
+            weight_local(piece, layer).wait()
+
+    for piece in HANDED:
+        weight_local(piece, c).start()
 
     ids = s.sample_ids[pl.ds(c, 1), :].astype(F32)
     count = [jnp.sum(jnp.where(ids == v, 1.0, 0.0), axis=-1, keepdims=True) for v in range(3)]
@@ -385,9 +391,10 @@
     cot_copy.wait()
     s.dy[...] = mm(s.perm[...], s.cot[...]).astype(BF)
 
+    need(c, *EARLY)
     links.met()
-    for name in WEIGHTS[:6]:
-        weight_copy(name, c).start()
+    for piece in EARLY:
+        weight_copy(piece, c).start()
 
     head0 = lax.broadcasted_iota(jnp.int32, (HALF, 128), 1) < HEAD_DIM
 
@@ -414,10 +421,10 @@
         ).wait()
 
     def forward(layer):
-        need(layer, "first_gain", "query", "key", "value")
         x = s.x[layer].astype(F32)
         r = rsqrt_mean(x)
         s.r1[layer] = r
+        pl.when(layer != c)(lambda: need(layer, *EARLY))
         a = (x * r * s.gain1[layer]).astype(BF)
         s.a[layer] = a
         for lo, hi in ((0, 512), (512, 1024), (1024, 1152)):
@@ -430,9 +437,8 @@
 
         @pl.when(layer == 0)
         def _():
-            for name in WEIGHTS[6:]:
-                weight_copy(name, c).start()
-
+            for piece in LATE:
+                weight_copy(piece, c).start()
 
         for pair, block in PARTS:
             at = pl.ds(block * HALF, HALF)
@@ -449,16 +455,15 @@
             s.inverse[layer, pair * 2 + block] = inverse
             s.o[layer, at, lanes(pair)] = (jnp.where(head0, outs[0], outs[1]) * inverse).astype(BF)
 
-        need(layer, "output", "second_gain")
+        need(layer, *LATE[:2])
         x1 = x + mm(s.o[layer], s.wo[layer])
         s.x1[layer] = x1
         r = rsqrt_mean(x1)
         s.r2[layer] = r
         s.b[layer] = (x1 * r * s.gain2[layer]).astype(BF)
-        need(layer, "gate", "up", "down")
 
     def hidden(layer, j):
-        at = pl.ds(j * CHUNK if isinstance(j, int) else pl.multiple_of(j * CHUNK, CHUNK), CHUNK)
+        at = pl.ds(j * CHUNK, CHUNK)
         b = s.b[layer]
         g = mm(b, s.wg[layer, :, at])
         u = mm(b, s.wu[layer, :, at])
@@ -477,8 +482,9 @@
         def _():
             s.acc[...] = s.x1[0]
 
-            @pl.loop(0, 4)
-            def _(j):
+            for j in range(4):
+                if j % 2 == 0:
+                    need(0, *LATE[2 + 3 * (j // 2) : 5 + 3 * (j // 2)])
                 at, g, u, sig = hidden(0, j)
                 f = (g * sig * u).astype(BF)
                 s.acc[...] += mm(f, s.wd[0, at, :])
@@ -522,6 +528,7 @@
     def made(u):
         links.core_copy(u).start()
 
+    need(1, *LATE[2:])
     s.gain_sum[0] = jnp.zeros((16, 128), F32)
 
     @pl.loop(0, 2)
@@ -625,12 +632,10 @@
 
     s.gains_out[...] = s.gain_sum[5, pl.ds(pl.multiple_of(c * 8, 8), 8), :]
 
-    @pl.loop(0, UNITS)
-    def _(u):
-        links.settle(u)
-
-    for index, name in enumerate(WEIGHTS):
-        weight_copy(name, c).wait_send()
+    links.settle()
+
+    for piece in HANDED:
+        weight_copy(piece, c).wait_send()
     output_settle(s.y_row.at[0], s.rows_out, s.y_sem)
     output_settle(s.dx_row.at[0], s.dx_out, s.dx_sem)
 
@@ -638,29 +643,25 @@
 def spread_kernel(*refs):
     s = types.SimpleNamespace(**dict(zip(SPREAD_NAMES, refs)))
 
-    def load(index, src, dst):
-        return pltpu.make_async_copy(src, dst, s.in_sem.at[index])
-
     def store(index, src, dst):
         return pltpu.make_async_copy(src, dst, s.out_sem.at[index])
 
-    unit_loads = [load(u, s.units.at[u], s.unit.at[u]) for u in range(6)]
-    dx_load = load(6, s.dx_in, s.dx)
-    rows_load = load(7, s.rows_in, s.rows)
-    stores = []
-    for u in (4, 5, 0, 1, 2, 3):
-        unit_loads[u].start()
-    rows_load.start()
-    dx_load.start()
+    stores = [store(0, s.rows_in, s.rows_out.at[0])]
+    stores[0].start()
+
+    @pl.loop(0, 2)
+    def _(row):
+        s.dx_wide[row] = s.dx_in[row].astype(F32)
+
+    stores.append(store(7, s.dx_wide, s.dx_out.at[0]))
+    stores[-1].start()
 
     def panels(u, first, size, wide, dst):
         for p in range(wide):
-            dst[:, p * 128 : (p + 1) * 128] = s.unit[u, pl.ds((first + p) * size, size), :].astype(F32)
+            dst[:, p * 128 : (p + 1) * 128] = s.units[u, pl.ds((first + p) * size, size), :].astype(F32)
 
     squares = ((4, 0, s.output), (4, 3, s.query), (5, 0, s.key), (5, 3, s.value))
     for index, (u, first, out) in enumerate(squares):
-        if first == 0:
-            unit_loads[u].wait()
         panels(u, first, DIM, 3, s.square.at[index])
         stores.append(store(1 + index, s.square.at[index], out.at[0]))
         stores[-1].start()
@@ -671,18 +672,6 @@
     stores.append(store(6, s.vectors.at[pl.ds(8, 1)], s.second))
     stores[-2].start()
     stores[-1].start()
-    rows_load.wait()
-    stores.append(store(0, s.rows, s.rows_out.at[0]))
-    stores[-1].start()
-    dx_load.wait()
-
-    @pl.loop(0, 2)
-    def _(row):
-        s.dx_wide[row] = s.dx[row].astype(F32)
-
-    stores.append(store(7, s.dx_wide, s.dx_out.at[0]))
-    stores[-1].start()
-
     def chunk_stores(u):
         at = pl.ds(pl.multiple_of(u * CHUNK, CHUNK), CHUNK)
         return (
@@ -693,7 +682,6 @@
 
     @pl.loop(0, 4)
     def _(u):
-        load(u, s.units.at[u], s.unit.at[u]).wait()
         panels(u, 0, CHUNK, 3, s.down_wide.at[u])
         panels(u, 2, DIM, 2, s.gate_wide.at[u])
         panels(u, 4, DIM, 2, s.up_wide.at[u])
@@ -723,16 +711,12 @@
     "down": ((1, FF, DIM), F32),
 }
 SPREAD_SCRATCH = {
-    "unit": pltpu.VMEM((6, UNIT, 128), BF),
-    "rows": pltpu.VMEM((2, SEQ, DIM), BF),
-    "dx": pltpu.VMEM((2, SEQ, DIM), BF),
     "dx_wide": pltpu.VMEM((2, SEQ, DIM), F32),
     "square": pltpu.VMEM((4, DIM, DIM), F32),
     "vectors": pltpu.VMEM((16, DIM), F32),
     "down_wide": pltpu.VMEM((4, CHUNK, DIM), F32),
     "gate_wide": pltpu.VMEM((4, DIM, CHUNK), F32),
     "up_wide": pltpu.VMEM((4, DIM, CHUNK), F32),
-    "in_sem": pltpu.SemaphoreType.DMA((8,)),
     "out_sem": pltpu.SemaphoreType.DMA((20,)),
 }
 SPREAD_NAMES = ["units", "rows_in", "dx_in", "gains_in", *SPREAD_OUTS, *SPREAD_SCRATCH]
@@ -742,11 +726,11 @@
     anywhere = pl.BlockSpec(memory_space=pl.ANY)
     return pl.pallas_call(
         spread_kernel,
-        in_specs=[anywhere] * 3 + [pl.BlockSpec(memory_space=pltpu.VMEM)],
+        in_specs=[pl.BlockSpec(memory_space=pltpu.VMEM)] * 4,
         out_specs=[anywhere] * len(SPREAD_OUTS),
         out_shape=[jax.ShapeDtypeStruct(*shape) for shape in SPREAD_OUTS.values()],
         scratch_shapes=list(SPREAD_SCRATCH.values()),
-        compiler_params=pltpu.CompilerParams(vmem_limit_bytes=62 * 2**20),
+        compiler_params=pltpu.CompilerParams(vmem_limit_bytes=40 * 2**20),
     )(units, rows_in, dx_in, gains)
 
 
@@ -755,10 +739,10 @@
     vmem = pl.BlockSpec(memory_space=pltpu.VMEM)
     inputs = ["tokens", "cotangent"] + ["in_" + name for name in WEIGHTS] + ["sample_ids"]
     outputs = {
-        "grads_out": jax.ShapeDtypeStruct((UNITS // 2, UNIT, 128), BF),
-        "rows_out": jax.ShapeDtypeStruct((2, SEQ, DIM), BF),
-        "dx_out": jax.ShapeDtypeStruct((2, SEQ, DIM), BF),
-        "gains_out": jax.ShapeDtypeStruct((8, 128), F32),
+        "grads_out": pltpu.VMEM((UNITS // 2, UNIT, 128), BF),
+        "rows_out": pltpu.VMEM((2, SEQ, DIM), BF),
+        "dx_out": pltpu.VMEM((2, SEQ, DIM), BF),
+        "gains_out": pltpu.VMEM((8, 128), F32),
     }
     dma = pltpu.SemaphoreType.DMA
     scratch = {
@@ -804,14 +788,14 @@
         "gain_sum": pltpu.VMEM((6, 16, 128), F32),
         "gain_land": pltpu.VMEM((5, 16, 128), F32),
         "in_sem": dma((2,)),
-        "w_sem": dma((2, len(WEIGHTS))),
-        "w_send": dma((len(WEIGHTS),)),
+        "w_sem": dma((2, len(HANDED))),
+        "w_send": dma((len(HANDED),)),
         "sent": dma((UNITS,)),
         "recv": dma((UNITS, 7)),
-        "core_sent": dma((UNITS,)),
+        "core_sent": dma,
         "core_recv": dma((UNITS,)),
-        "out_sent": dma((UNITS,)),
-        "out_recv": dma((UNITS,)),
+        "out_sent": dma,
+        "out_recv": dma,
         "gain_send": dma((5,)),
         "gain_recv": dma((5,)),
         "y_sem": dma((3,)),
@@ -825,7 +809,7 @@
         out_specs=[anywhere, anywhere, anywhere, vmem],
         scratch_shapes=list(scratch.values()),
         compiler_params=pltpu.CompilerParams(
-            collective_id=0, has_side_effects=True, vmem_limit_bytes=62 * 2**20
+            collective_id=0, has_side_effects=True, vmem_limit_bytes=52 * 2**20
         ),
         cost_estimate=pl.CostEstimate(flops=15 * 10**9, bytes_accessed=10**7, transcendentals=4 * 10**6),
     )(tokens, cotangent, *weights, sample_ids)

time: 89 us -> 83.6 us (0.939)
  Pallas kernels: 87.9 us -> 82.6 us
    pallas_call x1, Pallas kernels: 6.94 us -> 3.78 us  [spread(): pl.pallas_call(spread_kernel, in_specs=[pl.BlockSpec(memory_space=pltpu.V...]
    pallas_call x1, Pallas kernels: 81 us -> 78.8 us  [layers(): pl.pallas_call(functools.partial(kernel, names), out_shape=list(outputs.v...]
where the time goes in v4:
time: 83.6 us; the launch traced here: 83.5 us
  Pallas kernels  82.6 us (99%)
  between operations  0.84 us (1%)
    pallas_call x1, Pallas kernels, layers(): pl.pallas_call(functools.partial(kernel, names), out_shape=list(outputs.v...  78.8 us
    pallas_call x1, Pallas kernels, spread(): pl.pallas_call(spread_kernel, in_specs=[pl.BlockSpec(memory_space=pltpu.V...  3.78 us

profile of v4, /device:TPU:0, one launch (start us, length us, event | category | flops | bytes accessed | tf_op | source)
XLA Modules:
  0.0 83.5 jit_solution(5629776150649520495)
XLA Ops:
  0.6 78.8 %shard_map.203 = (bf16[6,2304,128]{2,1,0:T(8,128)(2,1)S(1)}, bf16[2,512,384]{2,1,0:T(8,128)(2,1)S(1)}, bf16[2,512,384]{2,1,0:T(8,128)(2,1)S(1)}, f32[8,128]{1,0:T(8,128)S(1)}) custom-call(bf16[2,512,384]{2,1,0:T(8,128)(2,1)} %refs_0_.1, bf16[2,512,384]{2,1,0:T(8,128)(2,1)} %refs_1_.1, f32[1,384]{1,0:T(1,128)} %refs_2_.1, bf16[1,384,384]{2,1,0:T(8,128)(2,1)} %refs_3_.1, ...), custom_call_target="tpu_custom_call" | custom-call | flops 15000000512 | bytes 10000000 | tf_op jit(solution)/shard_map/pallas_call | solution.py:805
  79.5 3.8 %shard_map.204 = (bf16[1,2,512,384]{3,2,1,0:T(8,128)(2,1)}, f32[1,2,512,384]{3,2,1,0:T(8,128)}, f32[1,384]{1,0:T(1,128)}, f32[1,384,384]{2,1,0:T(8,128)}, f32[1,...) custom-call(bf16[6,2304,128]{2,1,0:T(8,128)(2,1)S(1)} %get-tuple-ele, ...), custom_call_target="tpu_custom_call" | custom-call | tf_op jit(solution)/shard_map/pallas_call | solution.py:727

commit v5 on v4

--- a/solution.py
+++ b/solution.py
@@ -28,15 +28,15 @@
 PIECE = SHARE // 3
 SLOTS = 15
 WHEN = (
-    (2, 6, 11, 17, 21, 25, 34, 52),
-    (4, 8, 13, 17, 22, 28, 37, 58),
-    (6, 12, 16, 20, 24, 29, 40, 50),
-    (8, 12, 17, 21, 25, 35, 46, 61),
-    (14, 18, 22, 26, 31, 37, 44, 63),
-    (15, 19, 24, 28, 33, 40, 48, 69),
+    (2, 6, 11, 17, 21, 25, 34),
+    (4, 8, 13, 17, 22, 28, 37),
+    (6, 12, 16, 20, 24, 29, 40),
+    (8, 12, 17, 21, 25, 35, 46),
+    (14, 18, 22, 26, 31, 37, 44),
+    (15, 19, 24, 28, 33, 40, 48),
 )
 HALVES = (PIECE // 2, PIECE // 4, PIECE // 8)
-STAGES = 8
+STAGES = 7
 FLAT = (PIECE // 2, PIECE // 4, PIECE // 4, PIECE // 4, PIECE // 4, PIECE // 4, PIECE // 2)
 TALL = (PIECE // 2, PIECE // 4, PIECE // 8, PIECE // 8, PIECE // 8, PIECE // 4, PIECE // 2)
 FLAT_LAND = sum(FLAT[:4])
@@ -82,18 +82,19 @@
         p = lax.rem(z, 2)
         q = lax.div(z, 2)
         c = self.c
+        self.half = h = lax.rem(c + x + y + z, 2)
         self.middle = (z == 1) | (z == 2)
         self.end = (z == 0) | (z == 3)
         self.to_core = (1 - c, self.dp)
         step_x, step_y = 1 - 2 * x, 2 - 4 * y
-        self.to_x = (c, self.dp + step_x)
-        self.to_y = (c, self.dp + step_y)
-        self.to_p = (c, self.dp + 4 - 8 * p)
+        self.to_x = (1 - c, self.dp + step_x)
+        self.to_y = (1 - c, self.dp + step_y)
+        self.to_p = (1 - c, self.dp + 4 - 8 * p)
         self.to_q = (c, self.dp + 8 - 16 * q)
-        self.to_m = (c, self.dp + 4 - 8 * q)
+        self.to_m = (1 - c, self.dp + 4 - 8 * q)
         along_x, along_y, along_p = (x, self.to_x), (y, self.to_y), (p, self.to_p)
-        one = (x + c * (y - x), (c, self.dp + step_x + c * (step_y - step_x)))
-        two = (y + c * (x - y), (c, self.dp + step_y + c * (step_x - step_y)))
+        one = (x + h * (y - x), (1 - c, self.dp + step_x + h * (step_y - step_x)))
+        two = (y + h * (x - y), (1 - c, self.dp + step_y + h * (step_x - step_y)))
         orders = ((along_x, along_y), (along_y, along_x), (along_p, one, two))
         self.pieces = []
         for index, order in enumerate(orders):
@@ -104,7 +105,8 @@
 
     def meet(self):
         barrier = pltpu.get_barrier_semaphore()
-        for target in (self.to_core, self.to_x, self.to_y, self.to_p, self.to_q):
+        others = [(1 - self.c, target[1]) for target in (self.to_x, self.to_y, self.to_p)]
+        for target in (self.to_core, self.to_x, self.to_y, self.to_p, self.to_q, *others):
             pl.semaphore_signal(barrier, inc=1, device_id=target, device_id_type=MESH)
 
         @pl.when(self.middle)
@@ -116,11 +118,11 @@
 
         @pl.when(self.middle)
         def _():
-            pl.semaphore_wait(barrier, 6)
+            pl.semaphore_wait(barrier, 9)
 
         @pl.when(self.end)
         def _():
-            pl.semaphore_wait(barrier, 5)
+            pl.semaphore_wait(barrier, 8)
 
     def landing(self, index, step):
         table = FLAT if index < 2 else TALL
@@ -144,23 +146,38 @@
         pltpu.make_async_remote_copy(
             src_ref=src,
             dst_ref=s.land.at[u, self.landing(index, step)] if step < 4 else src,
-            send_sem=s.sent.at[u],
+            send_sem=s.sent,
             recv_sem=s.recv.at[u, step],
             device_id=target,
             device_id_type=MESH,
         ).start()
 
-    def wait(self, u, step, size, sent=False):
+    def finish(self, u, k, layer, piece):
+        _, order, starts = piece
+        s = self.s
+        src = s.done.at[u, rows(starts[1], HALVES[0])]
+        dst = s.grads_out.at[k, rows(self.half * SHARE + starts[1], HALVES[0])]
+
+        def hand(chip, sem):
+            pltpu.make_async_remote_copy(
+                src_ref=src, dst_ref=dst, send_sem=sem, recv_sem=s.out_recv,
+                device_id=(layer, chip), device_id_type=MESH,
+            ).start()
+
+        hand(order[0][1][1], s.sent)
+        pl.when(layer == self.c)(lambda: pltpu.make_async_copy(src, dst, s.out_sent).start())
+        pl.when(layer != self.c)(lambda: hand(self.dp, s.out_sent))
+
+    def wait(self, u, step, size):
         some = self.s.own.at[u, pl.ds(0, size)]
-        copy = pltpu.make_async_remote_copy(
+        pltpu.make_async_remote_copy(
             src_ref=some,
             dst_ref=some,
-            send_sem=self.s.sent.at[u],
+            send_sem=self.s.sent,
             recv_sem=self.s.recv.at[u, step],
             device_id=self.to_core,
             device_id_type=MESH,
-        )
-        copy.wait_send() if sent else copy.wait_recv()
+        ).wait_recv()
 
     def add(self, u, piece, step):
         index, order, starts = piece
@@ -175,7 +192,7 @@
 
     def core_copy(self, u):
         return pltpu.make_async_remote_copy(
-            src_ref=self.s.own.at[u, rows((1 - self.c) * SHARE, SHARE)],
+            src_ref=self.s.own.at[u, rows((1 - self.half) * SHARE, SHARE)],
             dst_ref=self.s.part.at[u],
             send_sem=self.s.core_sent,
             recv_sem=self.s.core_recv.at[u],
@@ -183,29 +200,13 @@
             device_id_type=MESH,
         )
 
-    def result(self, k):
-        return self.s.grads_out.at[k, rows(self.c * SHARE, SHARE)]
-
-    def result_local(self, u, k):
-        return pltpu.make_async_copy(self.s.done.at[u], self.result(k), self.s.out_sent)
-
-    def result_copy(self, u, k):
-        return pltpu.make_async_remote_copy(
-            src_ref=self.s.done.at[u],
-            dst_ref=self.result(k),
-            send_sem=self.s.out_sent,
-            recv_sem=self.s.out_recv,
-            device_id=self.to_core,
-            device_id_type=MESH,
-        )
-
     def stage(self, step, u, k, layer):
         s = self.s
         flat, tall = self.pieces[:2], self.pieces[2]
         both, everything = 2 * FLAT[2] + TALL[2], self.pieces
         if step == 0:
             self.core_copy(u).wait_recv()
-            s.part[u] = s.part[u] + s.own[u, rows(self.c * SHARE, SHARE)]
+            s.part[u] = s.part[u] + s.own[u, rows(self.half * SHARE, SHARE)]
             for piece in everything:
                 self.send(u, piece, 0)
         elif step == 1:
@@ -258,26 +259,24 @@
         elif step == 6:
             self.wait(u, 5, 3 * FLAT[5])
             for piece in everything:
-                self.send(u, piece, 6)
-        elif step == 7:
-            self.wait(u, 6, 3 * FLAT[6])
-            pl.when(layer == self.c)(lambda: self.result_local(u, k).start())
-            pl.when(layer != self.c)(lambda: self.result_copy(u, k).start())
-            sent = sum(TALL) + 2 * (FLAT[0] + FLAT[1] + FLAT[5] + FLAT[6])
-            pl.when(self.middle)(lambda: self.wait(u, 0, sent + 2 * (FLAT[3] + FLAT[4]), sent=True))
-            pl.when(self.end)(lambda: self.wait(u, 0, sent + 2 * FLAT[2], sent=True))
+                self.finish(u, k, layer, piece)
 
     def settle(self):
-        def whole(refs, send_sem, recv_sem):
+        def whole(units, size, send_sem):
+            some = self.s.own.at[pl.ds(0, units), pl.ds(0, size)]
             return pltpu.make_async_remote_copy(
-                src_ref=refs, dst_ref=refs, send_sem=send_sem, recv_sem=recv_sem,
+                src_ref=some, dst_ref=some, send_sem=send_sem, recv_sem=self.s.out_recv,
                 device_id=self.to_core, device_id_type=MESH,
             )
 
         s = self.s
-        whole(s.part, s.core_sent, s.out_recv).wait_send()
-        whole(s.done, s.out_sent, s.out_recv).wait_send()
-        whole(s.done.at[pl.ds(0, UNITS // 2)], s.out_sent, s.out_recv).wait_recv()
+        half = 3 * HALVES[0]
+        whole(UNITS, SHARE, s.core_sent).wait_send()
+        whole(UNITS, half, s.out_sent).wait_send()
+        sent = sum(TALL) + 2 * (FLAT[0] + FLAT[1] + FLAT[5] + FLAT[6])
+        pl.when(self.middle)(lambda: whole(UNITS, sent + 2 * (FLAT[3] + FLAT[4]), s.sent).wait_send())
+        pl.when(self.end)(lambda: whole(UNITS, sent + 2 * FLAT[2], s.sent).wait_send())
+        whole(UNITS // 2, 3 * half, s.out_sent).wait_recv()
 
     def sum_gains(self, step):
         s = self.s
@@ -361,6 +360,11 @@
 
     for piece in HANDED:
         weight_local(piece, c).start()
+
+    need(c, *EARLY)
+    links.met()
+    for piece in EARLY:
+        weight_copy(piece, c).start()
 
     ids = s.sample_ids[pl.ds(c, 1), :].astype(F32)
     count = [jnp.sum(jnp.where(ids == v, 1.0, 0.0), axis=-1, keepdims=True) for v in range(3)]
@@ -388,13 +392,11 @@
 
     token_copy.wait()
     s.x[0] = mm(s.perm[...], s.tok[...]).astype(BF)
+    for piece in LATE:
+        weight_copy(piece, c).start()
     cot_copy.wait()
     s.dy[...] = mm(s.perm[...], s.cot[...]).astype(BF)
 
-    need(c, *EARLY)
-    links.met()
-    for piece in EARLY:
-        weight_copy(piece, c).start()
 
     head0 = lax.broadcasted_iota(jnp.int32, (HALF, 128), 1) < HEAD_DIM
 
@@ -424,10 +426,12 @@
         x = s.x[layer].astype(F32)
         r = rsqrt_mean(x)
         s.r1[layer] = r
-        pl.when(layer != c)(lambda: need(layer, *EARLY))
+        pl.when(layer != c)(lambda: need(layer, *EARLY[:3]))
         a = (x * r * s.gain1[layer]).astype(BF)
         s.a[layer] = a
         for lo, hi in ((0, 512), (512, 1024), (1024, 1152)):
+            if lo == 512:
+                pl.when(layer != c)(lambda: need(layer, EARLY[3]))
             part = mm(a, s.wqkv[layer, :, lo:hi])
             if lo == 0:
                 s.qkv[layer, :, :DIM] = (part[:, :DIM] * HEAD_DIM ** (-0.5)).astype(BF)
@@ -435,22 +439,22 @@
             else:
                 s.qkv[layer, :, lo:hi] = part.astype(BF)
 
-        @pl.when(layer == 0)
-        def _():
-            for piece in LATE:
-                weight_copy(piece, c).start()
-
         for pair, block in PARTS:
             at = pl.ds(block * HALF, HALF)
-            q, k, v = [s.qkv[layer, at, lanes(pair, part)] for part in range(3)]
-            outs = []
+            q, k = [s.qkv[layer, at, lanes(pair, part)] for part in range(2)]
             for h in range(2):
                 score = mm_nt(q, of_head(k, h))
-                if block == 1:
-                    score = score + s.mask[...]
-                expo = jnp.exp(score - jnp.max(score, axis=-1, keepdims=True)).astype(BF)
-                s.e[layer, pair * 4 + block * 2 + h] = expo
-                outs.append(mm(expo, jnp.where(head0 if h == 0 else ~head0, v, jnp.ones_like(v))))
+                s.score[pair * 4 + block * 2 + h] = score + s.mask[...] if block == 1 else score
+        for head in range(2 * HEADS):
+            score = s.score[head]
+            s.e[layer, head] = jnp.exp(score - jnp.max(score, axis=-1, keepdims=True)).astype(BF)
+        for pair, block in PARTS:
+            at = pl.ds(block * HALF, HALF)
+            v = s.qkv[layer, at, lanes(pair, 2)]
+            outs = [
+                mm(s.e[layer, pair * 4 + block * 2 + h], jnp.where(head0 if h == 0 else ~head0, v, jnp.ones_like(v)))
+                for h in range(2)
+            ]
             inverse = 1.0 / pltpu.roll(jnp.where(head0, outs[1], outs[0]), HEAD_DIM, 1)
             s.inverse[layer, pair * 2 + block] = inverse
             s.o[layer, at, lanes(pair)] = (jnp.where(head0, outs[0], outs[1]) * inverse).astype(BF)
@@ -761,6 +765,7 @@
         "x": pltpu.VMEM((2, SEQ, DIM), BF),
         "a": pltpu.VMEM((2, SEQ, DIM), BF),
         "qkv": pltpu.VMEM((2, SEQ, 3 * DIM), BF),
+        "score": pltpu.VMEM((2 * HEADS, HALF, HALF), F32),
         "e": pltpu.VMEM((2, 2 * HEADS, HALF, HALF), BF),
         "inverse": pltpu.VMEM((2, HEADS, HALF, 128), F32),
         "f": pltpu.VMEM((SEQ, FF), BF),
@@ -790,8 +795,8 @@
         "in_sem": dma((2,)),
         "w_sem": dma((2, len(HANDED))),
         "w_send": dma((len(HANDED),)),
-        "sent": dma((UNITS,)),
-        "recv": dma((UNITS, 7)),
+        "sent": dma,
+        "recv": dma((UNITS, STAGES - 1)),
         "core_sent": dma,
         "core_recv": dma((UNITS,)),
         "out_sent": dma,
@@ -809,7 +814,7 @@
         out_specs=[anywhere, anywhere, anywhere, vmem],
         scratch_shapes=list(scratch.values()),
         compiler_params=pltpu.CompilerParams(
-            collective_id=0, has_side_effects=True, vmem_limit_bytes=52 * 2**20
+            collective_id=0, has_side_effects=True, vmem_limit_bytes=54 * 2**20
         ),
         cost_estimate=pl.CostEstimate(flops=15 * 10**9, bytes_accessed=10**7, transcendentals=4 * 10**6),
     )(tokens, cotangent, *weights, sample_ids)

time: 83.6 us -> 81.3 us (0.972)
  Pallas kernels: 82.6 us -> 80.3 us
    pallas_call x1, Pallas kernels: 78.8 us -> 76.5 us  [layers(): pl.pallas_call(functools.partial(kernel, names), out_shape=list(outputs.v...]
where the time goes in v5:
time: 81.3 us; the launch traced here: 81.1 us
  Pallas kernels  80.3 us (99%)
  between operations  0.84 us (1%)
    pallas_call x1, Pallas kernels, layers(): pl.pallas_call(functools.partial(kernel, names), out_shape=list(outputs.v...  76.5 us
    pallas_call x1, Pallas kernels, spread(): pl.pallas_call(spread_kernel, in_specs=[pl.BlockSpec(memory_space=pltpu.V...  3.78 us

profile of v5, /device:TPU:0, one launch (start us, length us, event | category | flops | bytes accessed | tf_op | source)
XLA Modules:
  0.0 81.1 jit_solution(4137528670631293918)
XLA Ops:
  0.6 76.5 %shard_map.203 = (bf16[6,2304,128]{2,1,0:T(8,128)(2,1)S(1)}, bf16[2,512,384]{2,1,0:T(8,128)(2,1)S(1)}, bf16[2,512,384]{2,1,0:T(8,128)(2,1)S(1)}, f32[8,128]{1,0:T(8,128)S(1)}) custom-call(bf16[2,512,384]{2,1,0:T(8,128)(2,1)} %refs_0_.1, bf16[2,512,384]{2,1,0:T(8,128)(2,1)} %refs_1_.1, f32[1,384]{1,0:T(1,128)} %refs_2_.1, bf16[1,384,384]{2,1,0:T(8,128)(2,1)} %refs_3_.1, ...), custom_call_target="tpu_custom_call" | custom-call | flops 15000000512 | bytes 10000000 | tf_op jit(solution)/shard_map/pallas_call | solution.py:810
  77.1 3.8 %shard_map.204 = (bf16[1,2,512,384]{3,2,1,0:T(8,128)(2,1)}, f32[1,2,512,384]{3,2,1,0:T(8,128)}, f32[1,384]{1,0:T(1,128)}, f32[1,384,384]{2,1,0:T(8,128)}, f32[1,...) custom-call(bf16[6,2304,128]{2,1,0:T(8,128)(2,1)S(1)} %get-tuple-ele, ...), custom_call_target="tpu_custom_call" | custom-call | tf_op jit(solution)/shard_map/pallas_call | solution.py:731

commit v6 on v5

--- a/solution.py
+++ b/solution.py
@@ -28,12 +28,12 @@
 PIECE = SHARE // 3
 SLOTS = 15
 WHEN = (
-    (2, 6, 11, 17, 21, 25, 34),
-    (4, 8, 13, 17, 22, 28, 37),
-    (6, 12, 16, 20, 24, 29, 40),
-    (8, 12, 17, 21, 25, 35, 46),
-    (14, 18, 22, 26, 31, 37, 44),
-    (15, 19, 24, 28, 33, 40, 48),
+    (2, 7, 12, 18, 22, 26, 35),
+    (4, 9, 14, 18, 23, 29, 38),
+    (6, 13, 17, 21, 25, 30, 41),
+    (8, 13, 18, 22, 26, 36, 47),
+    (14, 19, 23, 27, 32, 38, 45),
+    (15, 20, 25, 29, 34, 41, 49),
 )
 HALVES = (PIECE // 2, PIECE // 4, PIECE // 8)
 STAGES = 7
@@ -287,7 +287,7 @@
             return pltpu.make_async_remote_copy(
                 src_ref=total.at[index],
                 dst_ref=s.gain_land.at[index],
-                send_sem=s.gain_send.at[index],
+                send_sem=s.gain_send,
                 recv_sem=s.gain_recv.at[index],
                 device_id=targets[index],
                 device_id_type=MESH,
@@ -301,9 +301,15 @@
 
 
 WEIGHTS = ("first_gain", "query", "key", "value", "output", "second_gain", "gate", "up", "down")
-EARLY = (("first_gain", 0), ("query", 0), ("key", 0), ("value", 0))
-LATE = (("output", 0), ("second_gain", 0)) + tuple((name, half) for half in range(2) for name in ("gate", "up", "down"))
-HANDED = EARLY + LATE
+HANDED = (
+    (("first_gain", 0),),
+    (("query", 0), ("key", 0), ("value", 0)),
+    (("output", 0),),
+    (("second_gain", 0),),
+    (("gate", 0), ("up", 0), ("down", 0)),
+    (("gate", 1), ("up", 1), ("down", 1)),
+)
+EARLY, LATE = (0, 1), (2, 3, 4, 5)
 
 
 def kernel(names, *refs):
@@ -339,32 +345,36 @@
             return ref
         return ref.at[0, :, part] if name in ("gate", "up") else ref.at[0, part, :] if name == "down" else ref.at[0]
 
-    def weight_local(piece, layer):
-        sem = s.w_sem.at[layer, HANDED.index(piece)]
-        return pltpu.make_async_copy(source(*piece), place(*piece, layer), sem)
-
-    def weight_copy(piece, layer):
-        index = HANDED.index(piece)
-        return pltpu.make_async_remote_copy(
-            src_ref=place(*piece, layer) if piece in EARLY else source(*piece),
-            dst_ref=place(*piece, layer),
-            send_sem=s.w_send.at[index],
-            recv_sem=s.w_sem.at[layer, index],
-            device_id=links.to_core,
-            device_id_type=MESH,
-        )
-
-    def need(layer, *pieces):
-        for piece in pieces:
-            weight_local(piece, layer).wait()
-
-    for piece in HANDED:
-        weight_local(piece, c).start()
+    def weights_local(group, layer):
+        for piece in HANDED[group]:
+            pltpu.make_async_copy(source(*piece), place(*piece, layer), s.w_sem.at[layer, group]).start()
+
+    def weights_copy(group, layer):
+        for piece in HANDED[group]:
+            pltpu.make_async_remote_copy(
+                src_ref=place(*piece, layer) if group in EARLY else source(*piece),
+                dst_ref=place(*piece, layer),
+                send_sem=s.w_send.at[group],
+                recv_sem=s.w_sem.at[layer, group],
+                device_id=links.to_core,
+                device_id_type=MESH,
+            ).start()
+
+    def group_wait(group, sem):
+        some = (s.gain1.at[0], s.wqkv.at[0], s.wo.at[0], s.gain2.at[0], s.own.at[pl.ds(0, 2)], s.own.at[pl.ds(0, 2)])[group]
+        pltpu.make_async_copy(some, some, sem).wait()
+
+    def need(layer, *groups):
+        for group in groups:
+            group_wait(group, s.w_sem.at[layer, group])
+
+    for group in EARLY + LATE:
+        weights_local(group, c)
 
     need(c, *EARLY)
     links.met()
-    for piece in EARLY:
-        weight_copy(piece, c).start()
+    for group in EARLY:
+        weights_copy(group, c)
 
     ids = s.sample_ids[pl.ds(c, 1), :].astype(F32)
     count = [jnp.sum(jnp.where(ids == v, 1.0, 0.0), axis=-1, keepdims=True) for v in range(3)]
@@ -392,8 +402,8 @@
 
     token_copy.wait()
     s.x[0] = mm(s.perm[...], s.tok[...]).astype(BF)
-    for piece in LATE:
-        weight_copy(piece, c).start()
+    for group in LATE:
+        weights_copy(group, c)
     cot_copy.wait()
     s.dy[...] = mm(s.perm[...], s.cot[...]).astype(BF)
 
@@ -426,12 +436,10 @@
         x = s.x[layer].astype(F32)
         r = rsqrt_mean(x)
         s.r1[layer] = r
-        pl.when(layer != c)(lambda: need(layer, *EARLY[:3]))
+        pl.when(layer != c)(lambda: need(layer, *EARLY))
         a = (x * r * s.gain1[layer]).astype(BF)
         s.a[layer] = a
         for lo, hi in ((0, 512), (512, 1024), (1024, 1152)):
-            if lo == 512:
-                pl.when(layer != c)(lambda: need(layer, EARLY[3]))
             part = mm(a, s.wqkv[layer, :, lo:hi])
             if lo == 0:
                 s.qkv[layer, :, :DIM] = (part[:, :DIM] * HEAD_DIM ** (-0.5)).astype(BF)
@@ -488,7 +496,7 @@
 
             for j in range(4):
                 if j % 2 == 0:
-                    need(0, *LATE[2 + 3 * (j // 2) : 5 + 3 * (j // 2)])
+                    need(0, LATE[2 + j // 2])
                 at, g, u, sig = hidden(0, j)
                 f = (g * sig * u).astype(BF)
                 s.acc[...] += mm(f, s.wd[0, at, :])
@@ -638,8 +646,8 @@
 
     links.settle()
 
-    for piece in HANDED:
-        weight_copy(piece, c).wait_send()
+    for group in EARLY + LATE:
+        group_wait(group, s.w_send.at[group])
     output_settle(s.y_row.at[0], s.rows_out, s.y_sem)
     output_settle(s.dx_row.at[0], s.dx_out, s.dx_sem)
 
@@ -663,6 +671,22 @@
     def panels(u, first, size, wide, dst):
         for p in range(wide):
             dst[:, p * 128 : (p + 1) * 128] = s.units[u, pl.ds((first + p) * size, size), :].astype(F32)
+
+    def chunk_stores(u):
+        at = pl.ds(pl.multiple_of(u * CHUNK, CHUNK), CHUNK)
+        return (
+            store(8 + u, s.down_wide.at[u], s.down.at[0, at, :]),
+            store(12 + u, s.gate_wide.at[u], s.gate.at[0, :, at]),
+            store(16 + u, s.up_wide.at[u], s.up.at[0, :, at]),
+        )
+
+    @pl.loop(0, 4)
+    def _(u):
+        panels(u, 0, CHUNK, 3, s.down_wide.at[u])
+        panels(u, 2, DIM, 2, s.gate_wide.at[u])
+        panels(u, 4, DIM, 2, s.up_wide.at[u])
+        for one in chunk_stores(u):
+            one.start()
 
     squares = ((4, 0, s.output), (4, 3, s.query), (5, 0, s.key), (5, 3, s.value))
     for index, (u, first, out) in enumerate(squares):
@@ -676,22 +700,6 @@
     stores.append(store(6, s.vectors.at[pl.ds(8, 1)], s.second))
     stores[-2].start()
     stores[-1].start()
-    def chunk_stores(u):
-        at = pl.ds(pl.multiple_of(u * CHUNK, CHUNK), CHUNK)
-        return (
-            store(8 + u, s.down_wide.at[u], s.down.at[0, at, :]),
-            store(12 + u, s.gate_wide.at[u], s.gate.at[0, :, at]),
-            store(16 + u, s.up_wide.at[u], s.up.at[0, :, at]),
-        )
-
-    @pl.loop(0, 4)
-    def _(u):
-        panels(u, 0, CHUNK, 3, s.down_wide.at[u])
-        panels(u, 2, DIM, 2, s.gate_wide.at[u])
-        panels(u, 4, DIM, 2, s.up_wide.at[u])
-        for one in chunk_stores(u):
-            one.start()
-
     for one in stores:
         one.wait()
 
@@ -801,7 +809,7 @@
         "core_recv": dma((UNITS,)),
         "out_sent": dma,
         "out_recv": dma,
-        "gain_send": dma((5,)),
+        "gain_send": dma,
         "gain_recv": dma((5,)),
         "y_sem": dma((3,)),
         "dx_sem": dma((3,)),

time: 81.3 us -> 80.6 us (level)
  no operation moved by 1% of the time
where the time goes in v6:
time: 80.6 us; the launch traced here: 80.4 us
  Pallas kernels  79.6 us (99%)
  between operations  0.84 us (1%)
    pallas_call x1, Pallas kernels, layers(): pl.pallas_call(functools.partial(kernel, names), out_shape=list(outputs.v...  75.8 us
    pallas_call x1, Pallas kernels, spread(): pl.pallas_call(spread_kernel, in_specs=[pl.BlockSpec(memory_space=pltpu.V...  3.8 us

profile of v6, /device:TPU:0, one launch (start us, length us, event | category | flops | bytes accessed | tf_op | source)
XLA Modules:
  0.0 80.4 jit_solution(7208969842134222324)
XLA Ops:
  0.6 75.8 %shard_map.203 = (bf16[6,2304,128]{2,1,0:T(8,128)(2,1)S(1)}, bf16[2,512,384]{2,1,0:T(8,128)(2,1)S(1)}, bf16[2,512,384]{2,1,0:T(8,128)(2,1)S(1)}, f32[8,128]{1,0:T(8,128)S(1)}) custom-call(bf16[2,512,384]{2,1,0:T(8,128)(2,1)} %refs_0_.1, bf16[2,512,384]{2,1,0:T(8,128)(2,1)} %refs_1_.1, f32[1,384]{1,0:T(1,128)} %refs_2_.1, bf16[1,384,384]{2,1,0:T(8,128)(2,1)} %refs_3_.1, ...), custom_call_target="tpu_custom_call" | custom-call | flops 15000000512 | bytes 10000000 | tf_op jit(solution)/shard_map/pallas_call | solution.py:818
  76.4 3.8 %shard_map.204 = (bf16[1,2,512,384]{3,2,1,0:T(8,128)(2,1)}, f32[1,2,512,384]{3,2,1,0:T(8,128)}, f32[1,384]{1,0:T(1,128)}, f32[1,384,384]{2,1,0:T(8,128)}, f32[1,...) custom-call(bf16[6,2304,128]{2,1,0:T(8,128)(2,1)S(1)} %get-tuple-ele, ...), custom_call_target="tpu_custom_call" | custom-call | tf_op jit(solution)/shard_map/pallas_call | solution.py:739

commit v7 on v6

--- a/solution.py
+++ b/solution.py
@@ -32,8 +32,8 @@
     (4, 9, 14, 18, 23, 29, 38),
     (6, 13, 17, 21, 25, 30, 41),
     (8, 13, 18, 22, 26, 36, 47),
-    (14, 19, 23, 27, 32, 38, 45),
-    (15, 20, 25, 29, 34, 41, 49),
+    (14, 18, 22, 26, 31, 37, 44),
+    (15, 19, 24, 28, 33, 40, 48),
 )
 HALVES = (PIECE // 2, PIECE // 4, PIECE // 8)
 STAGES = 7

time: 80.6 us -> 80.1 us (level)
  no operation moved by 1% of the time
where the time goes in v7:
time: 80.1 us; the launch traced here: 79.9 us
  Pallas kernels  79 us (99%)
  between operations  0.84 us (1%)
    pallas_call x1, Pallas kernels, layers(): pl.pallas_call(functools.partial(kernel, names), out_shape=list(outputs.v...  75.2 us
    pallas_call x1, Pallas kernels, spread(): pl.pallas_call(spread_kernel, in_specs=[pl.BlockSpec(memory_space=pltpu.V...  3.8 us

profile of v7, /device:TPU:0, one launch (start us, length us, event | category | flops | bytes accessed | tf_op | source)
XLA Modules:
  0.0 79.9 jit_solution(15296501673421807785)
XLA Ops:
  0.6 75.2 %shard_map.203 = (bf16[6,2304,128]{2,1,0:T(8,128)(2,1)S(1)}, bf16[2,512,384]{2,1,0:T(8,128)(2,1)S(1)}, bf16[2,512,384]{2,1,0:T(8,128)(2,1)S(1)}, f32[8,128]{1,0:T(8,128)S(1)}) custom-call(bf16[2,512,384]{2,1,0:T(8,128)(2,1)} %refs_0_.1, bf16[2,512,384]{2,1,0:T(8,128)(2,1)} %refs_1_.1, f32[1,384]{1,0:T(1,128)} %refs_2_.1, bf16[1,384,384]{2,1,0:T(8,128)(2,1)} %refs_3_.1, ...), custom_call_target="tpu_custom_call" | custom-call | flops 15000000512 | bytes 10000000 | tf_op jit(solution)/shard_map/pallas_call | solution.py:818
  75.9 3.8 %shard_map.204 = (bf16[1,2,512,384]{3,2,1,0:T(8,128)(2,1)}, f32[1,2,512,384]{3,2,1,0:T(8,128)}, f32[1,384]{1,0:T(1,128)}, f32[1,384,384]{2,1,0:T(8,128)}, f32[1,...) custom-call(bf16[6,2304,128]{2,1,0:T(8,128)(2,1)S(1)} %get-tuple-ele, ...), custom_call_target="tpu_custom_call" | custom-call | tf_op jit(solution)/shard_map/pallas_call | solution.py:739

commit v8 on v7

--- a/solution.py
+++ b/solution.py
@@ -206,8 +206,10 @@
         both, everything = 2 * FLAT[2] + TALL[2], self.pieces
         if step == 0:
             self.core_copy(u).wait_recv()
-            s.part[u] = s.part[u] + s.own[u, rows(self.half * SHARE, SHARE)]
             for piece in everything:
+                begin = piece[0] * PIECE
+                here = pl.ds(begin, PIECE)
+                s.part[u, here] = s.part[u, here] + s.own[u, rows(self.half * SHARE + begin, PIECE)]
                 self.send(u, piece, 0)
         elif step == 1:
             self.wait(u, 0, 3 * FLAT[0])
@@ -216,14 +218,11 @@
                 self.send(u, piece, 1)
         elif step == 2:
             self.wait(u, 1, 3 * FLAT[1])
-            for piece in everything:
+            self.add(u, tall, 1)
+            self.send(u, tall, 2)
+            for piece in flat:
                 self.add(u, piece, 1)
-            self.send(u, tall, 2)
-
-            @pl.when(self.end)
-            def _():
-                for piece in flat:
-                    self.send(u, piece, 2)
+                pl.when(self.end)(functools.partial(self.send, u, piece, 2))
         elif step == 3:
             pl.when(self.middle)(lambda: self.wait(u, 2, both))
             pl.when(self.end)(lambda: self.wait(u, 2, TALL[2]))

time: 80.1 us -> 80.1 us (level)
  no operation moved by 1% of the time
where the time goes in v8:
time: 80.1 us; the launch traced here: 79.9 us
  Pallas kernels  79 us (99%)
  between operations  0.84 us (1%)
    pallas_call x1, Pallas kernels, layers(): pl.pallas_call(functools.partial(kernel, names), out_shape=list(outputs.v...  75.2 us
    pallas_call x1, Pallas kernels, spread(): pl.pallas_call(spread_kernel, in_specs=[pl.BlockSpec(memory_space=pltpu.V...  3.8 us

profile of v8, /device:TPU:0, one launch (start us, length us, event | category | flops | bytes accessed | tf_op | source)
XLA Modules:
  0.0 79.9 jit_solution(11526846732089697503)
XLA Ops:
  0.6 75.2 %shard_map.203 = (bf16[6,2304,128]{2,1,0:T(8,128)(2,1)S(1)}, bf16[2,512,384]{2,1,0:T(8,128)(2,1)S(1)}, bf16[2,512,384]{2,1,0:T(8,128)(2,1)S(1)}, f32[8,128]{1,0:T(8,128)S(1)}) custom-call(bf16[2,512,384]{2,1,0:T(8,128)(2,1)} %refs_0_.1, bf16[2,512,384]{2,1,0:T(8,128)(2,1)} %refs_1_.1, f32[1,384]{1,0:T(1,128)} %refs_2_.1, bf16[1,384,384]{2,1,0:T(8,128)(2,1)} %refs_3_.1, ...), custom_call_target="tpu_custom_call" | custom-call | flops 15000000512 | bytes 10000000 | tf_op jit(solution)/shard_map/pallas_call | solution.py:817
  75.9 3.8 %shard_map.204 = (bf16[1,2,512,384]{3,2,1,0:T(8,128)(2,1)}, f32[1,2,512,384]{3,2,1,0:T(8,128)}, f32[1,384]{1,0:T(1,128)}, f32[1,384,384]{2,1,0:T(8,128)}, f32[1,...) custom-call(bf16[6,2304,128]{2,1,0:T(8,128)(2,1)S(1)} %get-tuple-ele, ...), custom_call_target="tpu_custom_call" | custom-call | tf_op jit(solution)/shard_map/pallas_call | solution.py:738
